TPU v7x, 128 devices: a whole 4x4x4 slice. The times are simulated.
128 devices in a mesh: row: 8 (over x_hi, y), col: 8 (over z, core), sec: 2 (over x_lo).
Axes of the slice: x: 4 (x_hi: 2, x_lo: 2; x = x_hi * 2 + x_lo), y: 4, z: 4, core: 2. Of those that a mesh axis runs over, the one named last changes fastest.
Arguments:
- centers: float32 [3, 4096], replicated, may hold values from 0 to 4
- charge_sites: float32 [3, 65536], P(None, ('row', 'col', 'sec')), may hold values from 0 to 4
- charges: float32 [65536], P(('row', 'col', 'sec')), may hold values from -0.25 to 0.25
- amplitudes: float32 [6], replicated, may hold values from 0.05 to 0.3
- widths: float32 [6], replicated, may hold values from 0.2 to 0.5
- core_matrix: float32 [4096, 4096], P('row', ('col', 'sec')), may hold values from -0.9 to 0.9, as said below
- pattern: int32 [64, 64], P('row', ('col', 'sec')), may hold values from 0 to 1, as said below
Outputs:
- sign_matrix: float32 [4096, 4096], P('row', ('col', 'sec'))
Inputs may be any that keep to these rules, and one draw needn't show every extreme that they name: `pattern`: Symmetric; every diagonal block is 1. `core_matrix`: Symmetric, and zero outside the blocks that pattern marks.
All inputs are finite; a program needn't handle non-finite values.
Results may differ from a plain program's by a relative error of at most 0.0003.
Values sent between devices are 32-bit elements; how exact they have to be, the bound alone decides.
A program may use at most 64 MiB of HBM per device.

v0:
```python
import jax
import jax.numpy as jnp
from jax import lax
from jax.sharding import PartitionSpec as P

BLOCK = 64


def local_field(centers, charge_sites, charges, amplitudes, widths):
    center_count = centers.shape[1]
    block_len = min(512, center_count)
    blocks = centers.reshape(3, center_count // block_len, block_len).transpose(1, 0, 2)
    inverse = 1.0 / (widths * widths)

    def one_block(points):
        distance = (points[0][:, None] - charge_sites[0][None, :]) ** 2
        distance = distance + (points[1][:, None] - charge_sites[1][None, :]) ** 2
        distance = distance + (points[2][:, None] - charge_sites[2][None, :]) ** 2
        kernel = amplitudes[0] * jnp.exp(-distance * inverse[0])
        for term_number in range(1, amplitudes.shape[0]):
            kernel = kernel + amplitudes[term_number] * jnp.exp(-distance * inverse[term_number])
        return jnp.dot(
            kernel, charges, precision=lax.Precision.HIGHEST, preferred_element_type=jnp.float32
        )

    return lax.map(one_block, blocks).reshape(center_count)


def diagonal_piece(values, row_first, col_first, row_count, col_count):
    rows_id = row_first + lax.broadcasted_iota(jnp.int32, (row_count, col_count), 0)
    cols_id = col_first + lax.broadcasted_iota(jnp.int32, (row_count, col_count), 1)
    return jnp.where(rows_id == cols_id, values[:, None], 0.0)


def total_field(partial_value):
    return lax.psum(partial_value, ("row", "col", "sec"))


def column_panel(block_tile):
    return lax.all_gather(block_tile, "row", axis=0, tiled=True)


def fold_rows(block_tile, col_panel):
    return jnp.dot(
        lax.all_gather(block_tile, ("col", "sec"), axis=1, tiled=True),
        col_panel,
        precision=lax.Precision.HIGHEST,
        preferred_element_type=jnp.float32,
    )


def body(centers, charge_sites, charges, amplitudes, widths, core_matrix, pattern):
    row_count, col_count = core_matrix.shape
    row_first = lax.axis_index("row") * row_count
    col_first = lax.axis_index(("col", "sec")) * col_count
    element_mask = jnp.repeat(jnp.repeat(pattern, BLOCK, axis=0), BLOCK, axis=1).astype(jnp.float32)
    partial_value = local_field(centers, charge_sites, charges, amplitudes, widths)
    field = total_field(partial_value)
    row_field = lax.dynamic_slice_in_dim(field, row_first, row_count, 0)
    current = core_matrix + diagonal_piece(row_field, row_first, col_first, row_count, col_count)
    right_panel = column_panel(current)
    square = element_mask * fold_rows(current, right_panel)
    current = element_mask * (1.5 * current - 0.5 * fold_rows(square, right_panel))
    right_panel = column_panel(current)
    square = element_mask * fold_rows(current, right_panel)
    current = element_mask * (1.5 * current - 0.5 * fold_rows(square, right_panel))
    return current


def solution(mesh):
    return jax.shard_map(
        body,
        mesh=mesh,
        in_specs=(
            P(),
            P(None, ("row", "col", "sec")),
            P(("row", "col", "sec")),
            P(),
            P(),
            P("row", ("col", "sec")),
            P("row", ("col", "sec")),
        ),
        out_specs=P("row", ("col", "sec")),
        check_vma=False,
    )
```

profile of v0, /device:TPU:1, one launch (start us, length us, event | category | flops | bytes accessed | tf_op | source)
XLA Modules:
  0.0 618.9 jit_solution(3411371247247518321)
XLA Ops:
  7.2 111.2 %while.10 = (s32[]{:T(128)}, f32[8,512]{1,0:T(8,128)S(1)}, f32[6]{0:T(128)}, f32[8,3,512]{2,1,0:T(4,128)}, f32[3,512]{1,0:T(4,128)}, /*index=5*/f32[6]{0:T(128)S...) while((s32[]{:T(128)}, f32[8,512]{1,0:T(8,128)S(1)}, f32[6]{0:T(128)}, f32[8,3,512]{2,1,0:T(4,128)}, ...), condition=%wide.region_1.2_spmd, body=%wide.region_0.1_spmd.sunk | while | flops 9961476 | bytes 45357 | solution.py:26
  8.9 1.6 fusion.74
  10.4 10.6 %fusion.76 = f32[1,512]{1,0:T(1,128)S(1)} fusion(f32[512,1]{0,1:T(1,128)} %bitcast.89, f32[]{:T(128)} %bitcast.59, f32[]{:T(128)} %bitcast.60, f32[]{:T(128)} %bitcast.61, f32[]{:T(128)} %bitcast.62, f32[]{:T(128)} %bitcast.63, f32[]{:T(128)} %bitcast.64, f32[]{:T(128)} %bitcast.65, f32[]{:T(128)} %bitcast.66, f32[]{:T(128)} %bitcast.67, f32[]{:T(128)} %bitcast.68, ...), kind=kOutput, calls=%fused_computation.clone.1 | convolution fusion | flops 9961472 | bytes 16432 | tf_op jit(solution)/shard_map/while/body/eval_jaxpr/dot_general | solution.py:22
  22.8 1.6 fusion.74
  24.3 10.6 %fusion.76 = f32[1,512]{1,0:T(1,128)S(1)} fusion(f32[512,1]{0,1:T(1,128)} %bitcast.89, f32[]{:T(128)} %bitcast.59, f32[]{:T(128)} %bitcast.60, f32[]{:T(128)} %bitcast.61, f32[]{:T(128)} %bitcast.62, f32[]{:T(128)} %bitcast.63, f32[]{:T(128)} %bitcast.64, f32[]{:T(128)} %bitcast.65, f32[]{:T(128)} %bitcast.66, f32[]{:T(128)} %bitcast.67, f32[]{:T(128)} %bitcast.68, ...), kind=kOutput, calls=%fused_computation.clone.1 | convolution fusion | flops 9961472 | bytes 16432 | tf_op jit(solution)/shard_map/while/body/eval_jaxpr/dot_general | solution.py:22
  38.2 10.6 %fusion.76 = f32[1,512]{1,0:T(1,128)S(1)} fusion(f32[512,1]{0,1:T(1,128)} %bitcast.89, f32[]{:T(128)} %bitcast.59, f32[]{:T(128)} %bitcast.60, f32[]{:T(128)} %bitcast.61, f32[]{:T(128)} %bitcast.62, f32[]{:T(128)} %bitcast.63, f32[]{:T(128)} %bitcast.64, f32[]{:T(128)} %bitcast.65, f32[]{:T(128)} %bitcast.66, f32[]{:T(128)} %bitcast.67, f32[]{:T(128)} %bitcast.68, ...), kind=kOutput, calls=%fused_computation.clone.1 | convolution fusion | flops 9961472 | bytes 16432 | tf_op jit(solution)/shard_map/while/body/eval_jaxpr/dot_general | solution.py:22
  50.5 1.6 fusion.74
  52.1 10.6 %fusion.76 = f32[1,512]{1,0:T(1,128)S(1)} fusion(f32[512,1]{0,1:T(1,128)} %bitcast.89, f32[]{:T(128)} %bitcast.59, f32[]{:T(128)} %bitcast.60, f32[]{:T(128)} %bitcast.61, f32[]{:T(128)} %bitcast.62, f32[]{:T(128)} %bitcast.63, f32[]{:T(128)} %bitcast.64, f32[]{:T(128)} %bitcast.65, f32[]{:T(128)} %bitcast.66, f32[]{:T(128)} %bitcast.67, f32[]{:T(128)} %bitcast.68, ...), kind=kOutput, calls=%fused_computation.clone.1 | convolution fusion | flops 9961472 | bytes 16432 | tf_op jit(solution)/shard_map/while/body/eval_jaxpr/dot_general | solution.py:22
  66.0 10.6 %fusion.76 = f32[1,512]{1,0:T(1,128)S(1)} fusion(f32[512,1]{0,1:T(1,128)} %bitcast.89, f32[]{:T(128)} %bitcast.59, f32[]{:T(128)} %bitcast.60, f32[]{:T(128)} %bitcast.61, f32[]{:T(128)} %bitcast.62, f32[]{:T(128)} %bitcast.63, f32[]{:T(128)} %bitcast.64, f32[]{:T(128)} %bitcast.65, f32[]{:T(128)} %bitcast.66, f32[]{:T(128)} %bitcast.67, f32[]{:T(128)} %bitcast.68, ...), kind=kOutput, calls=%fused_computation.clone.1 | convolution fusion | flops 9961472 | bytes 16432 | tf_op jit(solution)/shard_map/while/body/eval_jaxpr/dot_general | solution.py:22
  78.3 1.6 fusion.74
  79.9 10.6 %fusion.76 = f32[1,512]{1,0:T(1,128)S(1)} fusion(f32[512,1]{0,1:T(1,128)} %bitcast.89, f32[]{:T(128)} %bitcast.59, f32[]{:T(128)} %bitcast.60, f32[]{:T(128)} %bitcast.61, f32[]{:T(128)} %bitcast.62, f32[]{:T(128)} %bitcast.63, f32[]{:T(128)} %bitcast.64, f32[]{:T(128)} %bitcast.65, f32[]{:T(128)} %bitcast.66, f32[]{:T(128)} %bitcast.67, f32[]{:T(128)} %bitcast.68, ...), kind=kOutput, calls=%fused_computation.clone.1 | convolution fusion | flops 9961472 | bytes 16432 | tf_op jit(solution)/shard_map/while/body/eval_jaxpr/dot_general | solution.py:22
  93.8 10.6 %fusion.76 = f32[1,512]{1,0:T(1,128)S(1)} fusion(f32[512,1]{0,1:T(1,128)} %bitcast.89, f32[]{:T(128)} %bitcast.59, f32[]{:T(128)} %bitcast.60, f32[]{:T(128)} %bitcast.61, f32[]{:T(128)} %bitcast.62, f32[]{:T(128)} %bitcast.63, f32[]{:T(128)} %bitcast.64, f32[]{:T(128)} %bitcast.65, f32[]{:T(128)} %bitcast.66, f32[]{:T(128)} %bitcast.67, f32[]{:T(128)} %bitcast.68, ...), kind=kOutput, calls=%fused_computation.clone.1 | convolution fusion | flops 9961472 | bytes 16432 | tf_op jit(solution)/shard_map/while/body/eval_jaxpr/dot_general | solution.py:22
  107.7 10.6 %fusion.76 = f32[1,512]{1,0:T(1,128)S(1)} fusion(f32[512,1]{0,1:T(1,128)} %bitcast.89, f32[]{:T(128)} %bitcast.59, f32[]{:T(128)} %bitcast.60, f32[]{:T(128)} %bitcast.61, f32[]{:T(128)} %bitcast.62, f32[]{:T(128)} %bitcast.63, f32[]{:T(128)} %bitcast.64, f32[]{:T(128)} %bitcast.65, f32[]{:T(128)} %bitcast.66, f32[]{:T(128)} %bitcast.67, f32[]{:T(128)} %bitcast.68, ...), kind=kOutput, calls=%fused_computation.clone.1 | convolution fusion | flops 9961472 | bytes 16432 | tf_op jit(solution)/shard_map/while/body/eval_jaxpr/dot_general | solution.py:22
  118.4 68.8 %psum.7 = f32[4096]{0:T(1024)S(1)} all-reduce(f32[4096]{0:T(1024)S(1)} %bitcast.80), channel_id=1, replica_groups=mesh['row'=8,'col'=8,'sec'=2] {'row','col','sec'}, use_global_device_ids=true, to_apply=%region_2.3 | all-reduce | flops 4096 | bytes 32768 | tf_op jit(solution)/shard_map/psum | solution.py:36
  189.2 66.4 %all-gather.9.cloned.1.call-done = f32[4096,256]{1,0:T(8,128)} async-done(((f32[512,256]{1,0:T(8,128)}), f32[4096,256]{1,0:T(8,128)}) %all-gather.9.cloned.1.call-update) | async-done | bytes 4194320 | tf_op jit(solution)/shard_map/all_gather | solution.py:40
  255.7 56.2 %all-gather.7.cloned.1.call-done = f32[512,4096]{1,0:T(8,128)} async-done(((f32[512,256]{1,0:T(8,128)}), f32[512,4096]{1,0:T(8,128)}) %all-gather.7.cloned.1.call-update) | async-done | bytes 8388624 | tf_op jit(solution)/shard_map/all_gather | solution.py:45
  311.9 11.6 %convolution_multiply_fusion.3 = f32[512,256]{0,1:T(8,128)} fusion(f32[512,256]{0,1:T(8,128)S(1)} %bitcast.77, f32[512,4096]{1,0:T(8,128)} %all-gather.7.cloned.1.call-done, f32[4096,256]{1,0:T(8,128)} %all-gather.9.cloned.1.call-done), kind=kOutput, calls=%fused_computation.57 | convolution fusion | flops 6442582016 | bytes 13631488 | tf_op jit(solution)/shard_map/dot_general | solution.py:44
  323.9 56.5 %all-gather.11.cloned.1.call-done = f32[512,4096]{0,1:T(8,128)} async-done(((f32[512,256]{0,1:T(8,128)}), f32[512,4096]{0,1:T(8,128)}) %all-gather.11.cloned.1.call-update) | async-done | bytes 8388624 | tf_op jit(solution)/shard_map/all_gather | solution.py:45
  380.4 17.7 %fusion.52 = f32[512,256]{1,0:T(8,128)} fusion(f32[512,256]{1,0:T(8,128)S(1)} %copy.10, f32[512,4096]{0,1:T(8,128)} %all-gather.11.cloned.1.call-done, f32[4096,256]{1,0:T(8,128)} %all-gather.9.cloned.1.call-done, f32[512,256]{1,0:T(8,128)S(1)} %copy-done.1), kind=kOutput, calls=%fused_computation.59 | convolution fusion | flops 6442975232 | bytes 14155776 | tf_op jit(solution)/shard_map/dot_general | solution.py:44
  399.0 70.8 %all-gather.15.cloned.1.call-done = f32[4096,256]{1,0:T(8,128)} async-done(((f32[512,256]{1,0:T(8,128)}), f32[4096,256]{1,0:T(8,128)}) %all-gather.15.cloned.1.call-update) | async-done | bytes 4194320 | tf_op jit(solution)/shard_map/all_gather | solution.py:40
  469.8 56.0 %all-gather.13.cloned.1.call-done = f32[512,4096]{1,0:T(8,128)} async-done(((f32[512,256]{1,0:T(8,128)}), f32[512,4096]{1,0:T(8,128)}) %all-gather.13.cloned.1.call-update) | async-done | bytes 8388624 | tf_op jit(solution)/shard_map/all_gather | solution.py:45
  525.9 11.5 %convolution_multiply_fusion.1 = f32[512,256]{0,1:T(8,128)} fusion(f32[512,256]{0,1:T(8,128)S(1)} %bitcast.79, f32[512,4096]{1,0:T(8,128)} %all-gather.13.cloned.1.call-done, f32[4096,256]{1,0:T(8,128)} %all-gather.15.cloned.1.call-done), kind=kOutput, calls=%fused_computation.55 | convolution fusion | flops 6442582016 | bytes 13631488 | tf_op jit(solution)/shard_map/dot_general | solution.py:44
  537.4 57.0 %all-gather.17.cloned.1.call-done = f32[512,4096]{0,1:T(8,128)} async-done(((f32[512,256]{0,1:T(8,128)}), f32[512,4096]{0,1:T(8,128)}) %all-gather.17.cloned.1.call-update) | async-done | bytes 8388624 | tf_op jit(solution)/shard_map/all_gather | solution.py:45
  594.3 17.7 %fusion.54 = f32[512,256]{1,0:T(8,128)} fusion(f32[512,256]{1,0:T(8,128)S(1)} %copy.10, f32[512,4096]{0,1:T(8,128)} %all-gather.17.cloned.1.call-done, f32[4096,256]{1,0:T(8,128)} %all-gather.15.cloned.1.call-done, f32[512,256]{1,0:T(8,128)S(1)} %copy-done), kind=kOutput, calls=%fused_computation.61 | convolution fusion | flops 6442975232 | bytes 14155776 | tf_op jit(solution)/shard_map/dot_general | solution.py:44
  (60 shorter events, 23.9 us)
Async XLA Ops:
  6.5 249.1 %all-gather.9.cloned.1.call-start = ((), (), s32[]{:S(2)}) async-start(), calls=%async_computation.1 | async-start | bytes 4718592 | tf_op jit(solution)/shard_map/all_gather | solution.py:40
  7.2 180.0 %copy-start.2 = (f32[512,256]{1,0:T(8,128)S(1)}, f32[512,256]{1,0:T(8,128)}, u32[]{:S(2)}) copy-start(f32[512,256]{1,0:T(8,128)} %param.14) | copy-start | bytes 1572868
  7.2 181.9 %copy-start.3 = (s32[8,4]{0,1:T(4,128)S(1)}, s32[8,4]{0,1:T(4,128)}, u32[]{:S(2)}) copy-start(s32[8,4]{0,1:T(4,128)} %param.15) | copy-start | bytes 388
  188.3 123.6 %all-gather.7.cloned.1.call-start = ((), (), s32[]{:S(2)}) async-start(), calls=%async_computation | async-start | bytes 8912896 | tf_op jit(solution)/shard_map/all_gather | solution.py:45
  189.0 191.4 %all-gather.11.cloned.1.call-start = ((), (), s32[]{:S(2)}) async-start(), calls=%async_computation.2 | async-start | bytes 8912896 | tf_op jit(solution)/shard_map/all_gather | solution.py:45
  311.9 68.6 %copy-start.1 = (f32[512,256]{1,0:T(8,128)S(1)}, f32[512,256]{1,0:T(8,128)}, u32[]{:S(2)}) copy-start(f32[512,256]{1,0:T(8,128)} %select_add_fusion) | copy-start | bytes 1572868
  323.5 146.4 %all-gather.15.cloned.1.call-start = ((), (), s32[]{:S(2)}) async-start(), calls=%async_computation.4 | async-start | bytes 4718592 | tf_op jit(solution)/shard_map/all_gather | solution.py:40
  398.1 127.7 %all-gather.13.cloned.1.call-start = ((), (), s32[]{:S(2)}) async-start(), calls=%async_computation.3 | async-start | bytes 8912896 | tf_op jit(solution)/shard_map/all_gather | solution.py:45
  398.7 195.6 %copy-start = (f32[512,256]{1,0:T(8,128)S(1)}, f32[512,256]{1,0:T(8,128)}, u32[]{:S(2)}) copy-start(f32[512,256]{1,0:T(8,128)} %fusion.52) | copy-start | bytes 1572868
  398.8 195.6 %all-gather.17.cloned.1.call-start = ((), (), s32[]{:S(2)}) async-start(), calls=%async_computation.5 | async-start | bytes 8912896 | tf_op jit(solution)/shard_map/all_gather | solution.py:45
Sparse Core Ops, SparseCore 0:
  188.4 67.2 all-gather.8
  257.3 54.4 all-gather.6
  323.6 56.7 all-gather.10
  398.3 71.5 all-gather.14
  471.4 54.4 all-gather.12
  537.5 56.7 all-gather.16
where the time goes:
time: 621 us; the launch traced here: 619 us
  waiting for transfers between devices  364 us (59%)
  matrix products  143 us (23%)
  blocking collectives  68.8 us (11%)
  local copies, waits for them, and re-layouts  26.6 us (4%)
  between operations  13.5 us (2%)
    all_gather x4, waiting for transfers between devices, fold_rows(): lax.all_gather(block_tile, ('col', 'sec'), axis=1, tiled=True)  226 us
    all_gather x2, waiting for transfers between devices, column_panel(): return lax.all_gather(block_tile, 'row', axis=0, tiled=True)  137 us
    dot_general x8, matrix products, one_block(): jnp.dot(kernel, charges, precision=lax.Precision.HIGHEST, preferred_eleme...  84.8 us
    psum x1, blocking collectives, total_field(): return lax.psum(partial_value, ('row', 'col', 'sec'))  68.8 us
    dot_general x4, matrix products, fold_rows(): jnp.dot(lax.all_gather(block_tile, ('col', 'sec'), axis=1, tiled=True), c...  58.4 us
    slice x16, local copies, waits for them, and re-layouts, one_block(): distance = (points[0][:, None] - charge_sites[0][None, :]) ** 2  13.1 us
    slice x8, local copies, waits for them, and re-layouts, one_block(): kernel = amplitudes[0] * jnp.exp(-distance * inverse[0])  12.6 us
  transfers between devices with their start and end apart: 6, of which 6 were waited for; matrix products, arithmetic and copies ran while one was open for 0% of the time, Pallas kernels for 0%

commit v1 on v0

v1 whole, which is shorter than its diff:
```python
import functools

import jax
import jax.numpy as jnp
from jax import lax
from jax.experimental import pallas as pl
from jax.experimental.pallas import tpu as pltpu
from jax.sharding import PartitionSpec as P

BLOCK = 64
STEPS = 2
ROWS, COLS, SECS = 8, 8, 2
TILES = COLS * SECS
CAP = 20
PAIRS = CAP // 2
HALF = PAIRS // 2
CHUNK = 128
LOG2E = 1.4426950408889634
MESH = pl.DeviceIdType.MESH
AXES = ("row", "col", "sec")


def local_field(centers, charge_sites, charges, amplitudes, widths):
    center_count = centers.shape[1]
    block_len = min(512, center_count)
    blocks = centers.reshape(3, center_count // block_len, block_len).transpose(1, 0, 2)
    inverse = 1.0 / (widths * widths)

    def one_block(points):
        distance = (points[0][:, None] - charge_sites[0][None, :]) ** 2
        distance = distance + (points[1][:, None] - charge_sites[1][None, :]) ** 2
        distance = distance + (points[2][:, None] - charge_sites[2][None, :]) ** 2
        kernel = amplitudes[0] * jnp.exp(-distance * inverse[0])
        for term_number in range(1, amplitudes.shape[0]):
            kernel = kernel + amplitudes[term_number] * jnp.exp(-distance * inverse[term_number])
        return jnp.dot(
            kernel, charges, precision=lax.Precision.HIGHEST, preferred_element_type=jnp.float32
        )

    return lax.map(one_block, blocks).reshape(center_count)


def diagonal_piece(values, row_first, col_first, row_count, col_count):
    rows_id = row_first + lax.broadcasted_iota(jnp.int32, (row_count, col_count), 0)
    cols_id = col_first + lax.broadcasted_iota(jnp.int32, (row_count, col_count), 1)
    return jnp.where(rows_id == cols_id, values[:, None], 0.0)


def column_panel(block_tile):
    return lax.all_gather(block_tile, "row", axis=0, tiled=True)


def fold_rows(block_tile, col_panel):
    return jnp.dot(
        lax.all_gather(block_tile, ("col", "sec"), axis=1, tiled=True),
        col_panel,
        precision=lax.Precision.HIGHEST,
        preferred_element_type=jnp.float32,
    )


def dense_body(centers, charge_sites, charges, amplitudes, widths, core_matrix, pattern):
    row_count, col_count = core_matrix.shape
    row_first = lax.axis_index("row") * row_count
    col_first = lax.axis_index(("col", "sec")) * col_count
    element_mask = jnp.repeat(jnp.repeat(pattern, BLOCK, axis=0), BLOCK, axis=1).astype(jnp.float32)
    field = lax.psum(local_field(centers, charge_sites, charges, amplitudes, widths), AXES)
    row_field = lax.dynamic_slice_in_dim(field, row_first, row_count, 0)
    current = core_matrix + diagonal_piece(row_field, row_first, col_first, row_count, col_count)
    for _ in range(STEPS):
        right_panel = column_panel(current)
        square = element_mask * fold_rows(current, right_panel)
        current = element_mask * (1.5 * current - 0.5 * fold_rows(square, right_panel))
    return current


def kernel(
    inv_ref,
    keep_ref,
    coef_ref,
    hdr_ref,
    centers_ref,
    sites_ref,
    charges_ref,
    core_ref,
    out_ref,
    flag_ref,
    rbuf,
    cbuf,
    a_hi,
    a_lo,
    b_hi,
    b_lo,
    acc,
    work,
    cur,
    sq,
    fan,
    f_own,
    f_one,
    f_two,
    f_three,
    f_sum,
    f_all,
    fi_col,
    hrow,
    hcol,
    trow,
    tcol,
    r_send,
    r_recv,
    c_send,
    c_recv,
    hr_send,
    hr_recv,
    hc_send,
    hc_recv,
    f1_send,
    f1_recv,
    f2_send,
    f2_recv,
    f3_send,
    f3_recv,
    t_sem,
):
    row, col, sec = lax.axis_index("row"), lax.axis_index("col"), lax.axis_index("sec")
    hi, y = row // 4, row % 4
    z, core = col // 2, col % 2
    me = 2 * col + sec

    sibling = (row, 2 * z + (1 - core), sec)
    x_peer = (row, col, 1 - sec)
    z_up = (row, 2 * ((z + 1) % 4) + core, sec)
    z_down = (row, 2 * ((z + 3) % 4) + core, sec)
    h_peer = ((row + 4) % 8, col, sec)
    y_up = (4 * hi + (y + 1) % 4, col, sec)
    y_down = (4 * hi + (y + 3) % 4, col, sec)

    def row_mate(d):
        other = (me + d) % TILES
        return (row, other // 2, other % 2)

    def col_mate(d):
        return ((row + d) % ROWS, col, sec)

    lane = lax.broadcasted_iota(jnp.int32, (BLOCK, 128), 1)
    sub = lax.broadcasted_iota(jnp.int32, (BLOCK, 128), 0)
    left = lane < BLOCK

    barrier = pltpu.get_barrier_semaphore()

    def greet_row(d, c):
        pl.semaphore_signal(barrier, inc=1, device_id=row_mate(d), device_id_type=MESH)
        return c

    def greet_col(d, c):
        pl.semaphore_signal(barrier, inc=1, device_id=col_mate(d), device_id_type=MESH)
        return c

    lax.fori_loop(1, TILES, greet_row, 0)
    lax.fori_loop(1, ROWS, greet_col, 0)


    def put(dst, number, value):
        dst[number] = value
        dst[16 + number] = pltpu.roll(value, BLOCK, 1)

    def compact(src, store):
        for u in range(PAIRS):
            value = jnp.where(left, src[inv_ref[0, 2 * u]], src[inv_ref[0, 2 * u + 1]])
            store(u, value)

    def unpack(load, table, tile, store):
        for u in range(PAIRS):
            value = load(u)
            work[u] = value
            work[PAIRS + 1 + u] = pltpu.roll(value, BLOCK, 1)
        for b in range(16):
            value = jnp.where(
                left, work[table[tile, 0, 2 * b]], work[table[tile, 0, 2 * b + 1]]
            )
            high = value.astype(jnp.bfloat16)
            low = (value - high.astype(jnp.float32)).astype(jnp.bfloat16)
            store(b, high, low)

    def unpack_row(p, tile):
        def store(b, high, low):
            at = (tile, pl.ds((b // 2) * BLOCK, BLOCK), pl.ds((b % 2) * 128, 128))
            a_hi[at] = high
            a_lo[at] = low

        unpack(lambda u: rbuf[p, tile, u], trow, tile, store)

    def unpack_col(step, tile):
        def store(b, high, low):
            at = (
                2 * tile + b // 8,
                pl.ds((b // 2 % 4) * BLOCK, BLOCK),
                pl.ds((b % 2) * 128, 128),
            )
            b_hi[at] = high
            b_lo[at] = low

        unpack(lambda u: cbuf[step, tile, u], tcol, tile, store)

    def fold(tile):
        dot = functools.partial(jnp.dot, preferred_element_type=jnp.float32)
        total = dot(a_hi[tile], b_hi[tile])
        total = total + dot(a_lo[tile], b_hi[tile])
        total = total + dot(a_hi[tile], b_lo[tile])
        acc[...] += total


    def halves(p, j):
        return [pl.ds(0, HALF), pl.ds(HALF, HALF)]

    def row_copy(p, tile, j, kind, h, dev):
        ref = rbuf.at[p, tile, pl.ds(h * HALF, HALF)]
        return pltpu.make_async_remote_copy(
            src_ref=ref,
            dst_ref=ref,
            send_sem=r_send.at[j, kind, h],
            recv_sem=r_recv.at[p, tile, h],
            device_id=dev,
            device_id_type=MESH,
        )

    def col_copy(s, tile, j, kind, h, dev):
        ref = cbuf.at[s, tile, pl.ds(h * HALF, HALF)]
        return pltpu.make_async_remote_copy(
            src_ref=ref,
            dst_ref=ref,
            send_sem=c_send.at[j, kind, h],
            recv_sem=c_recv.at[s, tile, h],
            device_id=dev,
            device_id_type=MESH,
        )

    def offset(k):
        return 3 * k - 5 * (k // 2) - 2 * (k // 3)

    def row_tile(j):
        return 4 * ((z + offset(j // 2)) % 4) + 2 * core + (sec + j) % 2

    def peer_tile(j):
        return 4 * ((z + offset(j // 2)) % 4) + 2 * (1 - core) + (sec + j) % 2

    def col_tile(j):
        return 4 * ((hi + j) % 2) + (y + offset(j // 2)) % 4

    def row_out(p, j, act):
        tile = row_tile(j)

        @pl.when(j < 2)
        def _():
            for h in range(2):
                act(row_copy(p, tile, j, 1, h, z_up))
                act(row_copy(p, tile, j, 2, h, z_down))

        @pl.when(j == 0)
        def _():
            for h in range(2):
                act(row_copy(p, tile, j, 3, h, x_peer))

        @pl.when(j // 2 == 1)
        def _():
            act(row_copy(p, tile, j, 1, 0, z_up))

        @pl.when(j // 2 == 2)
        def _():
            act(row_copy(p, tile, j, 2, 1, z_down))

        for h in range(2):
            act(row_copy(p, tile, j, 0, h, sibling))

    def col_out(s, j, act):
        tile = col_tile(j)

        @pl.when(j == 0)
        def _():
            for h in range(2):
                act(col_copy(s, tile, j, 2, h, h_peer))

        @pl.when(j < 2)
        def _():
            for h in range(2):
                act(col_copy(s, tile, j, 0, h, y_up))
                act(col_copy(s, tile, j, 1, h, y_down))

        @pl.when(j // 2 == 1)
        def _():
            act(col_copy(s, tile, j, 0, 0, y_up))

        @pl.when(j // 2 == 2)
        def _():
            act(col_copy(s, tile, j, 1, 1, y_down))

    def start(copy):
        copy.start()

    def drain(copy):
        copy.wait_send()

    def row_in(p, tile):
        for h in range(2):
            row_copy(p, tile, 0, 0, h, sibling).wait_recv()

    def col_in(s, tile):
        for h in range(2):
            col_copy(s, tile, 0, 0, h, y_up).wait_recv()

    def row_drain(p):
        def one(j, c):
            row_out(p, j, drain)
            return c

        lax.fori_loop(0, 8, one, 0)

    def col_drain(s):
        def one(j, c):
            col_out(s, j, drain)
            return c

        lax.fori_loop(0, 6, one, 0)

    def small(src, dst, send, recv, dev):
        return pltpu.make_async_remote_copy(
            src_ref=src, dst_ref=dst, send_sem=send, recv_sem=recv,
            device_id=dev, device_id_type=MESH,
        )

    def loop(first, last, f):
        def one(d, c):
            f(d)
            return c

        lax.fori_loop(first, last, one, 0)


    for b in range(16):
        put(cur, b, core_ref[pl.ds((b // 2) * BLOCK, BLOCK), pl.ds((b % 2) * 128, 128)])

    def keep_iterate(p, s):
        def store(u, value):
            rbuf[p, me, u] = value
            cbuf[s, row, u] = value

        compact(cur, store)

    keep_iterate(0, 0)
    work[PAIRS] = jnp.zeros((BLOCK, 128), jnp.float32)
    work[2 * PAIRS + 1] = jnp.zeros((BLOCK, 128), jnp.float32)
    hrow[me] = hdr_ref[...]
    hcol[row] = hdr_ref[...]

    pl.semaphore_wait(barrier, TILES - 1 + ROWS - 1)

    def hr_copy(d):
        return small(hdr_ref, hrow.at[me], hr_send.at[d], hr_recv.at[me], row_mate(d))

    def hc_copy(d):
        return small(hdr_ref, hcol.at[row], hc_send.at[d], hc_recv.at[row], col_mate(d))

    loop(1, TILES, lambda d: hr_copy(d).start())
    loop(1, ROWS, lambda d: hc_copy(d).start())

    def read_tables():
        def wait_row(d):
            other = (me + d) % TILES
            small(hdr_ref, hrow.at[other], hr_send.at[d], hr_recv.at[other], row_mate(d)).wait_recv()

        def wait_col(d):
            other = (row + d) % ROWS
            small(hdr_ref, hcol.at[other], hc_send.at[d], hc_recv.at[other], col_mate(d)).wait_recv()

        loop(1, TILES, wait_row)
        loop(1, ROWS, wait_col)
        one = pltpu.make_async_copy(hrow, trow, t_sem.at[0])
        two = pltpu.make_async_copy(hcol, tcol, t_sem.at[1])
        one.start()
        two.start()
        one.wait()
        two.wait()


    def spread_sites():
        for a in range(4):
            for c in range(4):
                if a < 3:
                    line = sites_ref[a : a + 1, c * 128 : (c + 1) * 128]
                else:
                    line = charges_ref[0:1, c * 128 : (c + 1) * 128]
                fan[a, c * 128 : (c + 1) * 128, :] = jnp.transpose(
                    jnp.broadcast_to(line, (128, 128))
                )

    def field_chunk(ch):
        at = pl.ds(pl.multiple_of(ch * CHUNK, CHUNK), CHUNK)
        px = centers_ref[0:1, at]
        py = centers_ref[1:2, at]
        pz = centers_ref[2:3, at]

        def some(m, total):
            part = pl.ds(m * 32, 32)
            dx = fan[0, part, :] - px
            dy = fan[1, part, :] - py
            dz = fan[2, part, :] - pz
            distance = dx * dx + dy * dy + dz * dz
            value = coef_ref[1, 0] * jnp.exp2(distance * coef_ref[0, 0])
            for g in range(1, 6):
                value = value + coef_ref[1, g] * jnp.exp2(distance * coef_ref[0, g])
            return total + value * fan[3, part, :]

        total = lax.fori_loop(0, 16, some, jnp.zeros((32, 128), jnp.float32), unroll=4)
        f_own[ch // 4, pl.ds(ch % 4, 1), :] = jnp.sum(total, axis=0, keepdims=True)

    def f1_copy(d):
        other = (row + d) % ROWS
        return small(f_own.at[other], f_one.at[row], f1_send.at[d], f1_recv.at[row], col_mate(d))

    def f1_wait(d):
        other = (row + d) % ROWS
        small(f_own.at[row], f_one.at[other], f1_send.at[d], f1_recv.at[other], col_mate(d)).wait_recv()

    def f2_copy(d):
        return small(f_sum, f_two.at[me], f2_send.at[d], f2_recv.at[me], row_mate(d))

    def f2_wait(d):
        other = (me + d) % TILES
        small(f_sum, f_two.at[other], f2_send.at[d], f2_recv.at[other], row_mate(d)).wait_recv()

    def f3_copy(d):
        return small(f_all, f_three.at[row], f3_send.at[d], f3_recv.at[row], col_mate(d))

    def f3_wait(d):
        other = (row + d) % ROWS
        small(f_all, f_three.at[other], f3_send.at[d], f3_recv.at[other], col_mate(d)).wait_recv()

    line8 = lax.broadcasted_iota(jnp.int32, (8, 128), 0)

    def field_first():
        f_one[row] = f_own[row]
        loop(1, ROWS, lambda d: f1_copy(d).start())

    def field_second():
        loop(1, ROWS, f1_wait)
        total = f_one[0]
        for r in range(1, ROWS):
            total = total + f_one[r]
        count = jnp.broadcast_to(hdr_ref[1:2, :], (8, 128)).astype(jnp.float32)
        total = jnp.where(line8 < 4, total, count)
        f_sum[...] = total
        f_two[me] = total
        loop(1, TILES, lambda d: f2_copy(d).start())

    def field_third():
        loop(1, TILES, f2_wait)
        total = f_two[0]
        most = f_two[0]
        for c in range(1, TILES):
            value = f_two[c]
            total = total + value
            most = jnp.maximum(most, value)
        total = jnp.where(line8 < 4, total, most)
        f_all[...] = total
        f_three[row] = total
        loop(1, ROWS, lambda d: f3_copy(d).start())

    def field_last():
        loop(1, ROWS, f3_wait)
        most = f_three[0]
        for r in range(1, ROWS):
            most = jnp.maximum(most, f_three[r])
        flag_ref[...] = most
        for c in range(4):
            line = f_three[row, c : c + 1, :]
            fi_col[c * 128 : (c + 1) * 128, :] = jnp.transpose(jnp.broadcast_to(line, (128, 128)))
        loop(1, ROWS, lambda d: f1_copy(d).wait_send())
        loop(1, TILES, lambda d: f2_copy(d).wait_send())
        loop(1, ROWS, lambda d: f3_copy(d).wait_send())
        loop(1, TILES, lambda d: hr_copy(d).wait_send())
        loop(1, ROWS, lambda d: hc_copy(d).wait_send())


    def one_step(step, carry):
        p = 2 * step
        first = step == 0

        def arrive(j):
            @pl.when(j > 0)
            def _():
                row_in(p, row_tile(j))

            row_out(p, j, start)

            @pl.when(j > 0)
            def _():
                col_in(step, col_tile(j))

            col_out(step, j, start)

            @pl.when(first)
            def _():
                @pl.when(j == 0)
                def _():
                    spread_sites()

                loop(4 * j, 4 * j + 4, field_chunk)

                @pl.when(j == 0)
                def _():
                    read_tables()

            unpack_row(p, row_tile(j))
            unpack_col(step, col_tile(j))

        loop(0, 8, arrive)

        @pl.when(first)
        def _():
            field_first()

        acc[...] = jnp.zeros_like(acc)

        def from_peer(j):
            fold(row_tile(j))

            @pl.when(first)
            def _():
                @pl.when(j == 2)
                def _():
                    field_second()

                @pl.when(j == 5)
                def _():
                    field_third()

            row_in(p, peer_tile(j))
            unpack_row(p, peer_tile(j))
            fold(peer_tile(j))

        loop(0, 8, from_peer)

        @pl.when(first)
        def _():
            field_last()

        scale = jnp.where(first, 1.0, 0.0)

        def pieces(b):
            at = (pl.ds((b // 2) * BLOCK, BLOCK), pl.ds((b % 2) * 128, 128))
            fi = scale * fi_col[pl.ds((b // 2) * BLOCK, BLOCK), :]
            fj = scale * f_three[me // 2, pl.ds((me % 2) * 2 + b % 2, 1), :]
            same = (sub + (512 * row + (b // 2) * BLOCK)) == (lane + (256 * me + (b % 2) * 128))
            return at, fi, fj, same

        for b in range(16):
            at, fi, fj, same = pieces(b)
            value = acc[at] + (fi + fj) * cur[b] + jnp.where(same, fi * fi, 0.0)
            put(sq, b, value)

        def store(u, value):
            rbuf[p + 1, me, u] = value

        compact(sq, store)
        row_drain(p)

        acc[...] = jnp.zeros_like(acc)

        def arrive_square(j):
            @pl.when(j > 0)
            def _():
                row_in(p + 1, row_tile(j))

            row_out(p + 1, j, start)
            unpack_row(p + 1, row_tile(j))
            fold(row_tile(j))

        loop(0, 8, arrive_square)

        def from_peer_square(j):
            row_in(p + 1, peer_tile(j))
            unpack_row(p + 1, peer_tile(j))
            fold(peer_tile(j))

        loop(0, 8, from_peer_square)

        for b in range(16):
            at, fi, fj, same = pieces(b)
            value = 1.5 * (cur[b] + jnp.where(same, fi, 0.0)) - 0.5 * (acc[at] + sq[b] * fj)
            put(cur, b, value)

        row_drain(p + 1)
        col_drain(step)

        @pl.when(step + 1 < STEPS)
        def _():
            keep_iterate(p + 2, step + 1)

        return carry

    lax.fori_loop(0, STEPS, one_step, 0)

    for b in range(16):
        at = (pl.ds((b // 2) * BLOCK, BLOCK), pl.ds((b % 2) * 128, 128))
        keep_left = keep_ref[b // 2, 2 * (b % 2)].astype(jnp.float32)
        keep_right = keep_ref[b // 2, 2 * (b % 2) + 1].astype(jnp.float32)
        out_ref[at] = cur[b] * jnp.where(left, keep_left, keep_right)


def tables(pattern):
    keep = pattern.reshape(32)
    number = lax.broadcasted_iota(jnp.int32, (32, 32), 0)
    other = lax.broadcasted_iota(jnp.int32, (32, 32), 1)
    before = jnp.sum(jnp.where(other < number, keep[None, :], 0), axis=1)
    block = lax.iota(jnp.int32, 32)
    turned = (before + block) % 2
    code = jnp.where((keep == 1) & (before < CAP), before // 2 + (PAIRS + 1) * turned, PAIRS)
    slot = lax.iota(jnp.int32, CAP)
    source = block[None, :] // 2 + 16 * ((block[None, :] + slot[:, None]) % 2)
    inverse = jnp.sum(
        jnp.where((keep[None, :] == 1) & (before[None, :] == slot[:, None]), source, 0), axis=1
    )
    header = jnp.zeros((8, 128), jnp.int32).at[0, :32].set(code)
    header = header.at[1, :].set(jnp.sum(keep))
    return header, inverse[None, :]


def body(centers, charge_sites, charges, amplitudes, widths, core_matrix, pattern):
    header, inverse = tables(pattern)
    coef = jnp.stack([-LOG2E / (widths * widths), amplitudes])
    vmem = pl.BlockSpec(memory_space=pltpu.VMEM)
    smem = pl.BlockSpec(memory_space=pltpu.SMEM)
    f32, bf16 = jnp.float32, jnp.bfloat16
    dma = pltpu.SemaphoreType.DMA
    out, flag = pl.pallas_call(
        kernel,
        out_shape=(
            jax.ShapeDtypeStruct((512, 256), f32),
            jax.ShapeDtypeStruct((8, 128), f32),
        ),
        in_specs=[smem, smem, smem, vmem, vmem, vmem, vmem, vmem],
        out_specs=(vmem, vmem),
        scratch_shapes=[
            pltpu.VMEM((4, TILES, PAIRS, BLOCK, 128), f32),
            pltpu.VMEM((2, ROWS, PAIRS, BLOCK, 128), f32),
            pltpu.VMEM((TILES, 512, 256), bf16),
            pltpu.VMEM((TILES, 512, 256), bf16),
            pltpu.VMEM((TILES, 256, 256), bf16),
            pltpu.VMEM((TILES, 256, 256), bf16),
            pltpu.VMEM((512, 256), f32),
            pltpu.VMEM((2 * PAIRS + 2, BLOCK, 128), f32),
            pltpu.VMEM((32, BLOCK, 128), f32),
            pltpu.VMEM((32, BLOCK, 128), f32),
            pltpu.VMEM((4, 512, 128), f32),
            pltpu.VMEM((ROWS, 8, 128), f32),
            pltpu.VMEM((ROWS, 8, 128), f32),
            pltpu.VMEM((TILES, 8, 128), f32),
            pltpu.VMEM((ROWS, 8, 128), f32),
            pltpu.VMEM((8, 128), f32),
            pltpu.VMEM((8, 128), f32),
            pltpu.VMEM((512, 128), f32),
            pltpu.VMEM((TILES, 8, 128), jnp.int32),
            pltpu.VMEM((ROWS, 8, 128), jnp.int32),
            pltpu.SMEM((TILES, 8, 128), jnp.int32),
            pltpu.SMEM((ROWS, 8, 128), jnp.int32),
            dma((8, 4, 2)),
            dma((4, TILES, 2)),
            dma((8, 3, 2)),
            dma((2, ROWS, 2)),
            dma((TILES,)),
            dma((TILES,)),
            dma((ROWS,)),
            dma((ROWS,)),
            dma((ROWS,)),
            dma((ROWS,)),
            dma((TILES,)),
            dma((TILES,)),
            dma((ROWS,)),
            dma((ROWS,)),
            dma((2,)),
        ],
        compiler_params=pltpu.CompilerParams(
            collective_id=0, has_side_effects=True, vmem_limit_bytes=58 * 1024 * 1024
        ),
    )(
        inverse,
        pattern,
        coef,
        header,
        centers,
        charge_sites,
        charges[None, :],
        core_matrix,
    )
    return lax.cond(
        flag[4, 0] > CAP,
        lambda: dense_body(
            centers, charge_sites, charges, amplitudes, widths, core_matrix, pattern
        ),
        lambda: out,
    )


def solution(mesh):
    return jax.shard_map(
        body,
        mesh=mesh,
        in_specs=(
            P(),
            P(None, AXES),
            P(AXES),
            P(),
            P(),
            P("row", ("col", "sec")),
            P("row", ("col", "sec")),
        ),
        out_specs=P("row", ("col", "sec")),
        check_vma=False,
    )
```

time: 621 us -> 188 us (0.30)
  waiting for transfers between devices: 364 us -> 0 us
  Pallas kernels: 0 us -> 163 us
  matrix products: 143 us -> 0 us
  blocking collectives: 68.8 us -> 0 us
  local copies, waits for them, and re-layouts: 26.6 us -> 4.29 us
    all_gather x6 -> x0, waiting for transfers between devices: 363 us -> none  [the longest x4 226 us: fold_rows(): lax.all_gather(block_tile, ('col', 'sec'), axis=1, tiled=True)]
    pallas_call x0 -> x1, Pallas kernels: none -> 163 us  [body(): pl.pallas_call(kernel, out_shape=(jax.ShapeDtypeStruct((512, 256), f32),...]
    dot_general x12 -> x0, matrix products: 143 us -> none  [the longest x8 84.8 us: one_block(): jnp.dot(kernel, charges, precision=lax.Precision.HIGHEST, preferred_eleme...]
    psum x1 -> x0, blocking collectives: 68.8 us -> none  [total_field(): return lax.psum(partial_value, ('row', 'col', 'sec'))]
    slice x24 -> x1, local copies, waits for them, and re-layouts: 25.7 us -> 1.19 us  [body(): flag[4, 0] > CAP]
  transfers between devices with their start and end apart: 6 -> 0, of which waited for: 6 -> 0; matrix products, arithmetic and copies ran while one was open for 0% -> 0% of each run, Pallas kernels for 0% -> 0%
where the time goes in v1:
time: 188 us; the launch traced here: 186 us
  Pallas kernels  163 us (87%)
  between operations  14.1 us (8%)
  other arithmetic  4.68 us (2%)
  local copies, waits for them, and re-layouts  4.29 us (2%)
    pallas_call x1, Pallas kernels, body(): pl.pallas_call(kernel, out_shape=(jax.ShapeDtypeStruct((512, 256), f32),...  163 us

profile of v1, /device:TPU:1, one launch (start us, length us, event | category | flops | bytes accessed | tf_op | source)
XLA Modules:
  0.0 186.1 jit_solution(1788129442851983036)
XLA Ops:
  6.5 1.3 reduce_sum.32
  7.9 0.6 broadcast.211
  8.5 0.7 divide_bitcast_fusion
  9.2 1.2 pad_maximum_fusion.coef_ref
  10.4 0.7 broadcast_compare_fusion
  11.1 0.1 copy.24
  11.2 0.1 eq.57
  11.3 0.8 copy.23.keep_ref
  12.0 0.0 copy-start.3
  12.0 0.1 broadcast_in_dim_reshape.4
  12.1 0.1 select_reduce_fusion
  12.2 0.7 fusion.59
  13.0 0.0 copy-done.3
  13.0 0.0 copy-start.5
  13.0 0.6 copy-done.5
  13.6 162.8 %shard_map.75 = (f32[512,256]{1,0:T(8,128)S(1)}, f32[8,128]{1,0:T(8,128)}) custom-call(s32[1,20]{1,0:T(1,128)} %bitcast.110, s32[8,4]{1,0:T(8,128)} %copy-done.3, f32[2,6]{1,0:T(2,128)} %pad_maximum_fusion.coef_ref, s32[8,128]{1,0:T(8,128)} %copy-done.5, f32[3,4096]{1,0:T(4,128)} %centers_ref.1, f32[3,512]{1,0:T(4,128)} %sites_ref.1, f32[1,512]{1,0:T(1,128)} %bitcast.108, ...), custom_call_target="tpu_custom_call" | custom-call | tf_op jit(solution)/shard_map/pallas_call | solution.py:636
  176.4 1.2 slice.91
  178.2 0.2 conditional.1
  178.5 0.8 copy.38
  (5 shorter events, 0.1 us)
Async XLA Ops:
  12.0 0.9 copy-start.3
  13.0 0.6 copy-start.5

commit v2 on v1

--- a/solution.py
+++ b/solution.py
@@ -75,10 +75,9 @@
 
 
 def kernel(
-    inv_ref,
     keep_ref,
-    coef_ref,
-    hdr_ref,
+    amp_ref,
+    width_ref,
     centers_ref,
     sites_ref,
     charges_ref,
@@ -103,8 +102,13 @@
     f_sum,
     f_all,
     fi_col,
+    hdr_ref,
+    inv_line,
+    coef_line,
     hrow,
     hcol,
+    inv_ref,
+    coef_ref,
     trow,
     tcol,
     r_send,
@@ -132,7 +136,7 @@
     x_peer = (row, col, 1 - sec)
     z_up = (row, 2 * ((z + 1) % 4) + core, sec)
     z_down = (row, 2 * ((z + 3) % 4) + core, sec)
-    h_peer = ((row + 4) % 8, col, sec)
+    across = ((row + 4) % 8, col, 1 - sec)
     y_up = (4 * hi + (y + 1) % 4, col, sec)
     y_down = (4 * hi + (y + 3) % 4, col, sec)
 
@@ -159,6 +163,33 @@
 
     lax.fori_loop(1, TILES, greet_row, 0)
     lax.fori_loop(1, ROWS, greet_col, 0)
+    pl.semaphore_signal(barrier, inc=1, device_id=across, device_id_type=MESH)
+
+
+    lane1 = lax.broadcasted_iota(jnp.int32, (1, 128), 1)
+    before = 0
+    codes = jnp.full((1, 128), PAIRS, jnp.int32)
+    blocks = jnp.zeros((1, 128), jnp.int32)
+    for b in range(32):
+        keep = keep_ref[b // 4, b % 4]
+        turned = (before + b) % 2
+        there = before // 2 + (PAIRS + 1) * turned
+        code = jnp.where((keep == 1) & (before < CAP), there, PAIRS)
+        codes = jnp.where(lane1 == b, code, codes)
+        at = jnp.where(keep == 1, before, 127)
+        blocks = jnp.where(lane1 == at, b // 2 + 16 * turned, blocks)
+        before = before + keep
+    hdr_ref[...] = jnp.where(lane1 == 127, before, codes)
+    inv_line[...] = jnp.where(lane1 < CAP, blocks, 0)
+    scale_line = jnp.zeros((1, 128), jnp.float32)
+    for g in range(6):
+        wide = jnp.full((1, 128), width_ref[g], jnp.float32)
+        scale_line = jnp.where(lane1 == g, -LOG2E / (wide * wide), scale_line)
+    coef_line[...] = scale_line
+    inv_copy = pltpu.make_async_copy(inv_line, inv_ref, t_sem.at[0])
+    coef_copy = pltpu.make_async_copy(coef_line, coef_ref, t_sem.at[1])
+    inv_copy.start()
+    coef_copy.start()
 
 
     def put(dst, number, value):
@@ -211,9 +242,6 @@
         acc[...] += total
 
 
-    def halves(p, j):
-        return [pl.ds(0, HALF), pl.ds(HALF, HALF)]
-
     def row_copy(p, tile, j, kind, h, dev):
         ref = rbuf.at[p, tile, pl.ds(h * HALF, HALF)]
         return pltpu.make_async_remote_copy(
@@ -236,64 +264,80 @@
             device_id_type=MESH,
         )
 
-    def offset(k):
-        return 3 * k - 5 * (k // 2) - 2 * (k // 3)
+
+    def mid(j):
+        return (j + 2) // 4 % 2
+
+    def hop(j):
+        return mid(j) * (3 - 2 * (j % 2)) + (1 - mid(j)) * 2 * (j // 6)
+
+    def swap(j):
+        return mid(j) * (j // 2 - 1) + (1 - mid(j)) * (j % 2)
 
     def row_tile(j):
-        return 4 * ((z + offset(j // 2)) % 4) + 2 * core + (sec + j) % 2
+        return 4 * ((z + hop(j)) % 4) + 2 * core + (sec + swap(j)) % 2
 
     def peer_tile(j):
-        return 4 * ((z + offset(j // 2)) % 4) + 2 * (1 - core) + (sec + j) % 2
+        return 4 * ((z + hop(j)) % 4) + 2 * (1 - core) + (sec + swap(j)) % 2
 
     def col_tile(j):
-        return 4 * ((hi + j) % 2) + (y + offset(j // 2)) % 4
-
-    def row_out(p, j, act):
+        return 4 * ((hi + swap(j)) % 2) + (y + hop(j)) % 4
+
+    def across_copy(p, s, h):
+        piece = pl.ds(h * HALF, HALF)
+        return pltpu.make_async_remote_copy(
+            src_ref=rbuf.at[p, row_tile(1), piece],
+            dst_ref=cbuf.at[s, row, piece],
+            send_sem=c_send.at[0, 2, h],
+            recv_sem=c_recv.at[s, row, h],
+            device_id=across,
+            device_id_type=MESH,
+        )
+
+    def row_out(p, j, h, act):
         tile = row_tile(j)
 
-        @pl.when(j < 2)
+        if h == 0:
+
+            @pl.when((j < 3) | ((j == 4) & (core == 0)))
+            def _():
+                act(row_copy(p, tile, j, 1, h, z_up))
+
+            @pl.when((j < 2) | ((j == 5) & (core == 1)))
+            def _():
+                act(row_copy(p, tile, j, 2, h, z_down))
+
+            @pl.when(j == 0)
+            def _():
+                act(row_copy(p, tile, j, 3, h, x_peer))
+
+        else:
+
+            @pl.when(j == 0)
+            def _():
+                act(row_copy(p, tile, j, 1, h, z_up))
+
+            @pl.when((j == 0) | (j == 3))
+            def _():
+                act(row_copy(p, tile, j, 2, h, z_down))
+
+            @pl.when((j == 0) | (j == 2) | (j == 3) | (j == 6))
+            def _():
+                act(row_copy(p, tile, j, 3, h, x_peer))
+
+        act(row_copy(p, tile, j, 0, h, sibling))
+
+    def col_out(s, j, h, act):
+        tile = col_tile(j)
+        up, down = ((j < 3) | (j == 4), j < 2) if h == 0 else (j < 2, (j < 2) | (j == 3) | (j == 5))
+
+        @pl.when(up)
         def _():
-            for h in range(2):
-                act(row_copy(p, tile, j, 1, h, z_up))
-                act(row_copy(p, tile, j, 2, h, z_down))
-
-        @pl.when(j == 0)
+            act(col_copy(s, tile, j, 0, h, y_up))
+
+        @pl.when(down)
         def _():
-            for h in range(2):
-                act(row_copy(p, tile, j, 3, h, x_peer))
-
-        @pl.when(j // 2 == 1)
-        def _():
-            act(row_copy(p, tile, j, 1, 0, z_up))
-
-        @pl.when(j // 2 == 2)
-        def _():
-            act(row_copy(p, tile, j, 2, 1, z_down))
-
-        for h in range(2):
-            act(row_copy(p, tile, j, 0, h, sibling))
-
-    def col_out(s, j, act):
-        tile = col_tile(j)
-
-        @pl.when(j == 0)
-        def _():
-            for h in range(2):
-                act(col_copy(s, tile, j, 2, h, h_peer))
-
-        @pl.when(j < 2)
-        def _():
-            for h in range(2):
-                act(col_copy(s, tile, j, 0, h, y_up))
-                act(col_copy(s, tile, j, 1, h, y_down))
-
-        @pl.when(j // 2 == 1)
-        def _():
-            act(col_copy(s, tile, j, 0, 0, y_up))
-
-        @pl.when(j // 2 == 2)
-        def _():
-            act(col_copy(s, tile, j, 1, 1, y_down))
+            act(col_copy(s, tile, j, 1, h, y_down))
 
     def start(copy):
         copy.start()
@@ -301,27 +345,29 @@
     def drain(copy):
         copy.wait_send()
 
-    def row_in(p, tile):
-        for h in range(2):
-            row_copy(p, tile, 0, 0, h, sibling).wait_recv()
-
-    def col_in(s, tile):
-        for h in range(2):
-            col_copy(s, tile, 0, 0, h, y_up).wait_recv()
+    def row_in(p, tile, h):
+        row_copy(p, tile, 0, 0, h, sibling).wait_recv()
+
+    def col_in(s, tile, h):
+        col_copy(s, tile, 0, 0, h, y_up).wait_recv()
 
     def row_drain(p):
         def one(j, c):
-            row_out(p, j, drain)
+            for h in range(2):
+                row_out(p, j, h, drain)
             return c
 
         lax.fori_loop(0, 8, one, 0)
 
-    def col_drain(s):
+    def col_drain(p, s):
         def one(j, c):
-            col_out(s, j, drain)
+            for h in range(2):
+                col_out(s, j, h, drain)
             return c
 
         lax.fori_loop(0, 6, one, 0)
+        for h in range(2):
+            across_copy(p, s, h).wait_send()
 
     def small(src, dst, send, recv, dev):
         return pltpu.make_async_remote_copy(
@@ -347,13 +393,15 @@
 
         compact(cur, store)
 
+    inv_copy.wait()
+    coef_copy.wait()
     keep_iterate(0, 0)
     work[PAIRS] = jnp.zeros((BLOCK, 128), jnp.float32)
     work[2 * PAIRS + 1] = jnp.zeros((BLOCK, 128), jnp.float32)
     hrow[me] = hdr_ref[...]
     hcol[row] = hdr_ref[...]
 
-    pl.semaphore_wait(barrier, TILES - 1 + ROWS - 1)
+    pl.semaphore_wait(barrier, TILES + ROWS - 1)
 
     def hr_copy(d):
         return small(hdr_ref, hrow.at[me], hr_send.at[d], hr_recv.at[me], row_mate(d))
@@ -406,9 +454,9 @@
             dy = fan[1, part, :] - py
             dz = fan[2, part, :] - pz
             distance = dx * dx + dy * dy + dz * dz
-            value = coef_ref[1, 0] * jnp.exp2(distance * coef_ref[0, 0])
+            value = amp_ref[0] * jnp.exp2(distance * coef_ref[0, 0])
             for g in range(1, 6):
-                value = value + coef_ref[1, g] * jnp.exp2(distance * coef_ref[0, g])
+                value = value + amp_ref[g] * jnp.exp2(distance * coef_ref[0, g])
             return total + value * fan[3, part, :]
 
         total = lax.fori_loop(0, 16, some, jnp.zeros((32, 128), jnp.float32), unroll=4)
@@ -447,7 +495,7 @@
         total = f_one[0]
         for r in range(1, ROWS):
             total = total + f_one[r]
-        count = jnp.broadcast_to(hdr_ref[1:2, :], (8, 128)).astype(jnp.float32)
+        count = jnp.broadcast_to(hdr_ref[...], (8, 128)).astype(jnp.float32)
         total = jnp.where(line8 < 4, total, count)
         f_sum[...] = total
         f_two[me] = total
@@ -471,7 +519,7 @@
         most = f_three[0]
         for r in range(1, ROWS):
             most = jnp.maximum(most, f_three[r])
-        flag_ref[...] = most
+        flag_ref[0, 0] = jnp.max(jnp.where(lane1 == 127, most[4:5, :], 0.0)).astype(jnp.int32)
         for c in range(4):
             line = f_three[row, c : c + 1, :]
             fi_col[c * 128 : (c + 1) * 128, :] = jnp.transpose(jnp.broadcast_to(line, (128, 128)))
@@ -487,59 +535,66 @@
         first = step == 0
 
         def arrive(j):
-            @pl.when(j > 0)
-            def _():
-                row_in(p, row_tile(j))
-
-            row_out(p, j, start)
-
-            @pl.when(j > 0)
-            def _():
-                col_in(step, col_tile(j))
-
-            col_out(step, j, start)
+            for h in range(2):
+
+                @pl.when(j > 0)
+                def _():
+                    row_in(p, row_tile(j), h)
+
+                row_out(p, j, h, start)
+
+                @pl.when(j == 1)
+                def _():
+                    across_copy(p, step, h).start()
+
+                @pl.when(j > 0)
+                def _():
+                    col_in(step, col_tile(j), h)
+
+                col_out(step, j, h, start)
 
             @pl.when(first)
             def _():
                 @pl.when(j == 0)
                 def _():
                     spread_sites()
-
-                loop(4 * j, 4 * j + 4, field_chunk)
-
-                @pl.when(j == 0)
-                def _():
+                    loop(0, 14, field_chunk)
                     read_tables()
+
+                @pl.when((j == 1) | (j == 2))
+                def _():
+                    loop(9 * j + 5, 9 * j + 14, field_chunk)
+
+                @pl.when(j == 2)
+                def _():
+                    field_first()
+
+                @pl.when(j == 4)
+                def _():
+                    field_second()
+
+                @pl.when(j == 6)
+                def _():
+                    field_third()
 
             unpack_row(p, row_tile(j))
             unpack_col(step, col_tile(j))
 
+            @pl.when(j > 0)
+            def _():
+                peer_in(p, j - 1)
+
+        def peer_in(q, j):
+            for h in range(2):
+                row_in(q, peer_tile(j), h)
+            unpack_row(q, peer_tile(j))
+
         loop(0, 8, arrive)
-
-        @pl.when(first)
-        def _():
-            field_first()
-
         acc[...] = jnp.zeros_like(acc)
-
-        def from_peer(j):
-            fold(row_tile(j))
-
-            @pl.when(first)
-            def _():
-                @pl.when(j == 2)
-                def _():
-                    field_second()
-
-                @pl.when(j == 5)
-                def _():
-                    field_third()
-
-            row_in(p, peer_tile(j))
-            unpack_row(p, peer_tile(j))
-            fold(peer_tile(j))
-
-        loop(0, 8, from_peer)
+        loop(0, 8, lambda j: fold(row_tile(j)))
+        loop(0, 7, lambda j: fold(peer_tile(j)))
+        peer_in(p, 7)
+        fold(peer_tile(7))
 
         @pl.when(first)
         def _():
@@ -568,22 +623,25 @@
         acc[...] = jnp.zeros_like(acc)
 
         def arrive_square(j):
-            @pl.when(j > 0)
-            def _():
-                row_in(p + 1, row_tile(j))
-
-            row_out(p + 1, j, start)
+            for h in range(2):
+
+                @pl.when(j > 0)
+                def _():
+                    row_in(p + 1, row_tile(j), h)
+
+                row_out(p + 1, j, h, start)
+
             unpack_row(p + 1, row_tile(j))
             fold(row_tile(j))
 
+            @pl.when(j > 0)
+            def _():
+                peer_in(p + 1, j - 1)
+                fold(peer_tile(j - 1))
+
         loop(0, 8, arrive_square)
-
-        def from_peer_square(j):
-            row_in(p + 1, peer_tile(j))
-            unpack_row(p + 1, peer_tile(j))
-            fold(peer_tile(j))
-
-        loop(0, 8, from_peer_square)
+        peer_in(p + 1, 7)
+        fold(peer_tile(7))
 
         for b in range(16):
             at, fi, fj, same = pieces(b)
@@ -591,7 +649,7 @@
             put(cur, b, value)
 
         row_drain(p + 1)
-        col_drain(step)
+        col_drain(p, step)
 
         @pl.when(step + 1 < STEPS)
         def _():
@@ -608,27 +666,7 @@
         out_ref[at] = cur[b] * jnp.where(left, keep_left, keep_right)
 
 
-def tables(pattern):
-    keep = pattern.reshape(32)
-    number = lax.broadcasted_iota(jnp.int32, (32, 32), 0)
-    other = lax.broadcasted_iota(jnp.int32, (32, 32), 1)
-    before = jnp.sum(jnp.where(other < number, keep[None, :], 0), axis=1)
-    block = lax.iota(jnp.int32, 32)
-    turned = (before + block) % 2
-    code = jnp.where((keep == 1) & (before < CAP), before // 2 + (PAIRS + 1) * turned, PAIRS)
-    slot = lax.iota(jnp.int32, CAP)
-    source = block[None, :] // 2 + 16 * ((block[None, :] + slot[:, None]) % 2)
-    inverse = jnp.sum(
-        jnp.where((keep[None, :] == 1) & (before[None, :] == slot[:, None]), source, 0), axis=1
-    )
-    header = jnp.zeros((8, 128), jnp.int32).at[0, :32].set(code)
-    header = header.at[1, :].set(jnp.sum(keep))
-    return header, inverse[None, :]
-
-
 def body(centers, charge_sites, charges, amplitudes, widths, core_matrix, pattern):
-    header, inverse = tables(pattern)
-    coef = jnp.stack([-LOG2E / (widths * widths), amplitudes])
     vmem = pl.BlockSpec(memory_space=pltpu.VMEM)
     smem = pl.BlockSpec(memory_space=pltpu.SMEM)
     f32, bf16 = jnp.float32, jnp.bfloat16
@@ -637,10 +675,10 @@
         kernel,
         out_shape=(
             jax.ShapeDtypeStruct((512, 256), f32),
-            jax.ShapeDtypeStruct((8, 128), f32),
+            jax.ShapeDtypeStruct((1, 1), jnp.int32),
         ),
-        in_specs=[smem, smem, smem, vmem, vmem, vmem, vmem, vmem],
-        out_specs=(vmem, vmem),
+        in_specs=[smem, smem, smem, vmem, vmem, vmem, vmem],
+        out_specs=(vmem, smem),
         scratch_shapes=[
             pltpu.VMEM((4, TILES, PAIRS, BLOCK, 128), f32),
             pltpu.VMEM((2, ROWS, PAIRS, BLOCK, 128), f32),
@@ -660,10 +698,15 @@
             pltpu.VMEM((8, 128), f32),
             pltpu.VMEM((8, 128), f32),
             pltpu.VMEM((512, 128), f32),
-            pltpu.VMEM((TILES, 8, 128), jnp.int32),
-            pltpu.VMEM((ROWS, 8, 128), jnp.int32),
-            pltpu.SMEM((TILES, 8, 128), jnp.int32),
-            pltpu.SMEM((ROWS, 8, 128), jnp.int32),
+            pltpu.VMEM((1, 128), jnp.int32),
+            pltpu.VMEM((1, 128), jnp.int32),
+            pltpu.VMEM((1, 128), f32),
+            pltpu.VMEM((TILES, 1, 128), jnp.int32),
+            pltpu.VMEM((ROWS, 1, 128), jnp.int32),
+            pltpu.SMEM((1, 128), jnp.int32),
+            pltpu.SMEM((1, 128), f32),
+            pltpu.SMEM((TILES, 1, 128), jnp.int32),
+            pltpu.SMEM((ROWS, 1, 128), jnp.int32),
             dma((8, 4, 2)),
             dma((4, TILES, 2)),
             dma((8, 3, 2)),
@@ -684,17 +727,16 @@
             collective_id=0, has_side_effects=True, vmem_limit_bytes=58 * 1024 * 1024
         ),
     )(
-        inverse,
         pattern,
-        coef,
-        header,
+        amplitudes,
+        widths,
         centers,
         charge_sites,
         charges[None, :],
         core_matrix,
     )
     return lax.cond(
-        flag[4, 0] > CAP,
+        flag[0, 0] > CAP,
         lambda: dense_body(
             centers, charge_sites, charges, amplitudes, widths, core_matrix, pattern
         ),

time: 188 us -> 161 us (0.86)
  Pallas kernels: 163 us -> 144 us
  other arithmetic: 4.68 us -> 0 us
  local copies, waits for them, and re-layouts: 4.29 us -> 2.14 us
    pallas_call x1, Pallas kernels: 163 us -> 144 us  [body(): pl.pallas_call(kernel, out_shape=(jax.ShapeDtypeStruct((512, 256), f32),...]
    reduce_sum x3 -> x0, other arithmetic: 2.1 us -> none  [the longest x1 1.32 us: tables(): header = header.at[1, :].set(jnp.sum(keep))]
where the time goes in v2:
time: 161 us
  Pallas kernels  144 us (89%)
  between operations  14 us (9%)
  local copies, waits for them, and re-layouts  2.14 us (1%)
    pallas_call x1, Pallas kernels, body(): pl.pallas_call(kernel, out_shape=(jax.ShapeDtypeStruct((512, 256), f32),...  144 us

profile of v2, /device:TPU:1, one launch (start us, length us, event | category | flops | bytes accessed | tf_op | source)
XLA Modules:
  0.0 160.5 jit_solution(12442100777416659581)
XLA Ops:
  6.5 1.3 copy.14.keep_ref
  7.9 144.2 %shard_map.75 = (f32[512,256]{1,0:T(8,128)S(1)}, s32[1,1]{1,0:T(1,128)}) custom-call(s32[8,4]{1,0:T(8,128)} %copy.14.keep_ref, f32[6]{0:T(128)} %amp_ref.1, f32[6]{0:T(128)} %width_ref.1, f32[3,4096]{1,0:T(4,128)} %centers_ref.1, f32[3,512]{1,0:T(4,128)} %sites_ref.1, f32[1,512]{1,0:T(1,128)} %bitcast.91, f32[512,256]{1,0:T(8,128)} %core_ref.1), custom_call_target="tpu_custom_call" | custom-call | tf_op jit(solution)/shard_map/pallas_call | solution.py:674
  152.7 0.2 conditional.1
  152.9 0.8 copy.26

commit v3 on v2

--- a/solution.py
+++ b/solution.py
@@ -12,69 +12,15 @@
 ROWS, COLS, SECS = 8, 8, 2
 TILES = COLS * SECS
 CAP = 20
-PAIRS = CAP // 2
-HALF = PAIRS // 2
+FULL = 32
 CHUNK = 128
 LOG2E = 1.4426950408889634
 MESH = pl.DeviceIdType.MESH
 AXES = ("row", "col", "sec")
 
 
-def local_field(centers, charge_sites, charges, amplitudes, widths):
-    center_count = centers.shape[1]
-    block_len = min(512, center_count)
-    blocks = centers.reshape(3, center_count // block_len, block_len).transpose(1, 0, 2)
-    inverse = 1.0 / (widths * widths)
-
-    def one_block(points):
-        distance = (points[0][:, None] - charge_sites[0][None, :]) ** 2
-        distance = distance + (points[1][:, None] - charge_sites[1][None, :]) ** 2
-        distance = distance + (points[2][:, None] - charge_sites[2][None, :]) ** 2
-        kernel = amplitudes[0] * jnp.exp(-distance * inverse[0])
-        for term_number in range(1, amplitudes.shape[0]):
-            kernel = kernel + amplitudes[term_number] * jnp.exp(-distance * inverse[term_number])
-        return jnp.dot(
-            kernel, charges, precision=lax.Precision.HIGHEST, preferred_element_type=jnp.float32
-        )
-
-    return lax.map(one_block, blocks).reshape(center_count)
-
-
-def diagonal_piece(values, row_first, col_first, row_count, col_count):
-    rows_id = row_first + lax.broadcasted_iota(jnp.int32, (row_count, col_count), 0)
-    cols_id = col_first + lax.broadcasted_iota(jnp.int32, (row_count, col_count), 1)
-    return jnp.where(rows_id == cols_id, values[:, None], 0.0)
-
-
-def column_panel(block_tile):
-    return lax.all_gather(block_tile, "row", axis=0, tiled=True)
-
-
-def fold_rows(block_tile, col_panel):
-    return jnp.dot(
-        lax.all_gather(block_tile, ("col", "sec"), axis=1, tiled=True),
-        col_panel,
-        precision=lax.Precision.HIGHEST,
-        preferred_element_type=jnp.float32,
-    )
-
-
-def dense_body(centers, charge_sites, charges, amplitudes, widths, core_matrix, pattern):
-    row_count, col_count = core_matrix.shape
-    row_first = lax.axis_index("row") * row_count
-    col_first = lax.axis_index(("col", "sec")) * col_count
-    element_mask = jnp.repeat(jnp.repeat(pattern, BLOCK, axis=0), BLOCK, axis=1).astype(jnp.float32)
-    field = lax.psum(local_field(centers, charge_sites, charges, amplitudes, widths), AXES)
-    row_field = lax.dynamic_slice_in_dim(field, row_first, row_count, 0)
-    current = core_matrix + diagonal_piece(row_field, row_first, col_first, row_count, col_count)
-    for _ in range(STEPS):
-        right_panel = column_panel(current)
-        square = element_mask * fold_rows(current, right_panel)
-        current = element_mask * (1.5 * current - 0.5 * fold_rows(square, right_panel))
-    return current
-
-
 def kernel(
+    cap,
     keep_ref,
     amp_ref,
     width_ref,
@@ -127,6 +73,8 @@
     f3_recv,
     t_sem,
 ):
+    pairs = cap // 2
+    half = pairs // 2
     row, col, sec = lax.axis_index("row"), lax.axis_index("col"), lax.axis_index("sec")
     hi, y = row // 4, row % 4
     z, core = col // 2, col % 2
@@ -168,19 +116,19 @@
 
     lane1 = lax.broadcasted_iota(jnp.int32, (1, 128), 1)
     before = 0
-    codes = jnp.full((1, 128), PAIRS, jnp.int32)
+    codes = jnp.full((1, 128), pairs, jnp.int32)
     blocks = jnp.zeros((1, 128), jnp.int32)
     for b in range(32):
         keep = keep_ref[b // 4, b % 4]
         turned = (before + b) % 2
-        there = before // 2 + (PAIRS + 1) * turned
-        code = jnp.where((keep == 1) & (before < CAP), there, PAIRS)
+        there = before // 2 + (pairs + 1) * turned
+        code = jnp.where((keep == 1) & (before < cap), there, pairs)
         codes = jnp.where(lane1 == b, code, codes)
         at = jnp.where(keep == 1, before, 127)
         blocks = jnp.where(lane1 == at, b // 2 + 16 * turned, blocks)
         before = before + keep
     hdr_ref[...] = jnp.where(lane1 == 127, before, codes)
-    inv_line[...] = jnp.where(lane1 < CAP, blocks, 0)
+    inv_line[...] = jnp.where(lane1 < cap, blocks, 0)
     scale_line = jnp.zeros((1, 128), jnp.float32)
     for g in range(6):
         wide = jnp.full((1, 128), width_ref[g], jnp.float32)
@@ -197,15 +145,15 @@
         dst[16 + number] = pltpu.roll(value, BLOCK, 1)
 
     def compact(src, store):
-        for u in range(PAIRS):
+        for u in range(pairs):
             value = jnp.where(left, src[inv_ref[0, 2 * u]], src[inv_ref[0, 2 * u + 1]])
             store(u, value)
 
     def unpack(load, table, tile, store):
-        for u in range(PAIRS):
+        for u in range(pairs):
             value = load(u)
             work[u] = value
-            work[PAIRS + 1 + u] = pltpu.roll(value, BLOCK, 1)
+            work[pairs + 1 + u] = pltpu.roll(value, BLOCK, 1)
         for b in range(16):
             value = jnp.where(
                 left, work[table[tile, 0, 2 * b]], work[table[tile, 0, 2 * b + 1]]
@@ -220,7 +168,7 @@
             a_hi[at] = high
             a_lo[at] = low
 
-        unpack(lambda u: rbuf[p, tile, u], trow, tile, store)
+        unpack(lambda u: rbuf[p % 2, tile, u], trow, tile, store)
 
     def unpack_col(step, tile):
         def store(b, high, low):
@@ -243,7 +191,7 @@
 
 
     def row_copy(p, tile, j, kind, h, dev):
-        ref = rbuf.at[p, tile, pl.ds(h * HALF, HALF)]
+        ref = rbuf.at[p % 2, tile, pl.ds(h * half, half)]
         return pltpu.make_async_remote_copy(
             src_ref=ref,
             dst_ref=ref,
@@ -254,7 +202,7 @@
         )
 
     def col_copy(s, tile, j, kind, h, dev):
-        ref = cbuf.at[s, tile, pl.ds(h * HALF, HALF)]
+        ref = cbuf.at[s, tile, pl.ds(h * half, half)]
         return pltpu.make_async_remote_copy(
             src_ref=ref,
             dst_ref=ref,
@@ -284,9 +232,9 @@
         return 4 * ((hi + swap(j)) % 2) + (y + hop(j)) % 4
 
     def across_copy(p, s, h):
-        piece = pl.ds(h * HALF, HALF)
+        piece = pl.ds(h * half, half)
         return pltpu.make_async_remote_copy(
-            src_ref=rbuf.at[p, row_tile(1), piece],
+            src_ref=rbuf.at[p % 2, row_tile(1), piece],
             dst_ref=cbuf.at[s, row, piece],
             send_sem=c_send.at[0, 2, h],
             recv_sem=c_recv.at[s, row, h],
@@ -294,54 +242,66 @@
             device_id_type=MESH,
         )
 
-    def row_out(p, j, h, act):
-        tile = row_tile(j)
-
-        if h == 0:
-
-            @pl.when((j < 3) | ((j == 4) & (core == 0)))
-            def _():
-                act(row_copy(p, tile, j, 1, h, z_up))
-
-            @pl.when((j < 2) | ((j == 5) & (core == 1)))
-            def _():
-                act(row_copy(p, tile, j, 2, h, z_down))
-
-            @pl.when(j == 0)
-            def _():
-                act(row_copy(p, tile, j, 3, h, x_peer))
-
+    row_plan = {
+        (0, 0): (1, 2, 3, 0),
+        (0, 1): (1, 2, 3, 0),
+        (1, 0): (0,),
+        (1, 1): (1, 2, 0),
+        (2, 0): (1, 3, 0),
+        (2, 1): (0,),
+        (3, 0): (3, 0),
+        (3, 1): (2, 0),
+        (4, 0): (0,),
+        (4, 1): (1, 0),
+        (5, 0): (0,),
+        (5, 1): (2, 0),
+        (6, 0): (3, 0),
+        (6, 1): (0,),
+        (7, 0): (0,),
+        (7, 1): (0,),
+    }
+    col_plan = {
+        (0, 0): (0, 1),
+        (0, 1): (0, 1),
+        (1, 0): (0, 1),
+        (1, 1): (0, 1),
+        (2, 0): (0,),
+        (3, 1): (1,),
+        (4, 0): (0,),
+        (5, 1): (1,),
+    }
+    row_to = (sibling, z_up, z_down, x_peer)
+    col_to = (y_up, y_down)
+
+    def row_act(p, j, h, kind, act):
+        def go():
+            act(row_copy(p, row_tile(j), j, kind, h, row_to[kind]))
+
+        if j in (4, 5) and kind > 0:
+            pl.when(core == j - 4)(go)
         else:
-
-            @pl.when(j == 0)
-            def _():
-                act(row_copy(p, tile, j, 1, h, z_up))
-
-            @pl.when((j == 0) | (j == 3))
-            def _():
-                act(row_copy(p, tile, j, 2, h, z_down))
-
-            @pl.when((j == 0) | (j == 2) | (j == 3) | (j == 6))
-            def _():
-                act(row_copy(p, tile, j, 3, h, x_peer))
-
-        act(row_copy(p, tile, j, 0, h, sibling))
-
-    def col_out(s, j, h, act):
-        tile = col_tile(j)
-        up, down = ((j < 3) | (j == 4), j < 2) if h == 0 else (j < 2, (j < 2) | (j == 3) | (j == 5))
-
-        @pl.when(up)
-        def _():
-            act(col_copy(s, tile, j, 0, h, y_up))
-
-        @pl.when(down)
-        def _():
-            act(col_copy(s, tile, j, 1, h, y_down))
+            go()
+
+    def col_act(s, j, h, kind, act):
+        act(col_copy(s, col_tile(j), j, kind, h, col_to[kind]))
 
     def start(copy):
         copy.start()
 
+    def row_pass(p, *pieces):
+        for j, h in pieces:
+            if j > 0:
+                row_in(p, row_tile(j), h)
+            for kind in row_plan[j, h]:
+                row_act(p, j, h, kind, start)
+
+    def col_pass(s, *pieces):
+        for j, h in pieces:
+            if j > 0:
+                col_in(s, col_tile(j), h)
+            for kind in col_plan[j, h]:
+                col_act(s, j, h, kind, start)
+
     def drain(copy):
         copy.wait_send()
 
@@ -352,22 +312,14 @@
         col_copy(s, tile, 0, 0, h, y_up).wait_recv()
 
     def row_drain(p):
-        def one(j, c):
-            for h in range(2):
-                row_out(p, j, h, drain)
-            return c
-
-        lax.fori_loop(0, 8, one, 0)
-
-    def col_drain(p, s):
-        def one(j, c):
-            for h in range(2):
-                col_out(s, j, h, drain)
-            return c
-
-        lax.fori_loop(0, 6, one, 0)
-        for h in range(2):
-            across_copy(p, s, h).wait_send()
+        for (j, h), kinds in row_plan.items():
+            for kind in kinds:
+                row_act(p, j, h, kind, drain)
+
+    def col_drain(s):
+        for (j, h), kinds in col_plan.items():
+            for kind in kinds:
+                col_act(s, j, h, kind, drain)
 
     def small(src, dst, send, recv, dev):
         return pltpu.make_async_remote_copy(
@@ -388,7 +340,7 @@
 
     def keep_iterate(p, s):
         def store(u, value):
-            rbuf[p, me, u] = value
+            rbuf[p % 2, me, u] = value
             cbuf[s, row, u] = value
 
         compact(cur, store)
@@ -396,8 +348,8 @@
     inv_copy.wait()
     coef_copy.wait()
     keep_iterate(0, 0)
-    work[PAIRS] = jnp.zeros((BLOCK, 128), jnp.float32)
-    work[2 * PAIRS + 1] = jnp.zeros((BLOCK, 128), jnp.float32)
+    work[pairs] = jnp.zeros((BLOCK, 128), jnp.float32)
+    work[2 * pairs + 1] = jnp.zeros((BLOCK, 128), jnp.float32)
     hrow[me] = hdr_ref[...]
     hcol[row] = hdr_ref[...]
 
@@ -534,71 +486,86 @@
         p = 2 * step
         first = step == 0
 
-        def arrive(j):
-            for h in range(2):
-
-                @pl.when(j > 0)
-                def _():
-                    row_in(p, row_tile(j), h)
-
-                row_out(p, j, h, start)
-
-                @pl.when(j == 1)
-                def _():
-                    across_copy(p, step, h).start()
-
-                @pl.when(j > 0)
-                def _():
-                    col_in(step, col_tile(j), h)
-
-                col_out(step, j, h, start)
-
+        def rows_open(q, from_, to_):
+            loop(from_, to_, lambda j: unpack_row(q, row_tile(j)))
+
+        def peers_open(q, from_, to_):
+            def one(j):
+                for h in range(2):
+                    row_in(q, peer_tile(j), h)
+                unpack_row(q, peer_tile(j))
+
+            loop(from_, to_, one)
+
+        def once(*acts):
             @pl.when(first)
             def _():
-                @pl.when(j == 0)
-                def _():
-                    spread_sites()
-                    loop(0, 14, field_chunk)
-                    read_tables()
-
-                @pl.when((j == 1) | (j == 2))
-                def _():
-                    loop(9 * j + 5, 9 * j + 14, field_chunk)
-
-                @pl.when(j == 2)
-                def _():
-                    field_first()
-
-                @pl.when(j == 4)
-                def _():
-                    field_second()
-
-                @pl.when(j == 6)
-                def _():
-                    field_third()
-
-            unpack_row(p, row_tile(j))
-            unpack_col(step, col_tile(j))
-
-            @pl.when(j > 0)
+                for act in acts:
+                    act()
+
+        def chunks(from_, to_):
+            return lambda: loop(from_, to_, field_chunk)
+
+        for h in range(2):
+            row_pass(p, (0, h))
+            col_pass(step, (0, h))
+        once(spread_sites, chunks(0, 9), read_tables)
+        rows_open(p, 0, 1)
+        unpack_col(step, col_tile(0))
+        col_pass(step, (2, 0))
+        row_pass(p, (2, 0), (3, 0), (1, 0))
+        across_copy(p, step, 0).start()
+        once(chunks(9, 18))
+        row_pass(p, (3, 1), (1, 1))
+        across_copy(p, step, 1).start()
+        col_pass(step, (3, 1))
+        row_pass(p, (2, 1))
+        once(chunks(18, 26))
+        rows_open(p, 1, 4)
+        col_pass(step, (1, 0))
+        row_pass(p, (6, 0))
+        col_pass(step, (1, 1))
+        once(chunks(26, 32), field_first)
+        unpack_col(step, col_tile(1))
+        row_pass(p, (4, 0), (6, 1), (4, 1))
+        peers_open(p, 0, 3)
+        row_pass(p, (5, 1), (5, 0))
+        col_in(step, col_tile(2), 1)
+        col_in(step, col_tile(3), 0)
+        loop(2, 4, lambda j: unpack_col(step, col_tile(j)))
+        col_pass(step, (4, 0), (5, 1))
+        once(field_second)
+        rows_open(p, 4, 7)
+        row_pass(p, (7, 0), (7, 1))
+        peers_open(p, 3, 6)
+        rows_open(p, 7, 8)
+        col_in(step, col_tile(4), 1)
+        col_in(step, col_tile(5), 0)
+        for h in range(2):
+            col_in(step, col_tile(6), h)
+        loop(4, 7, lambda j: unpack_col(step, col_tile(j)))
+        once(field_third)
+        peers_open(p, 6, 7)
+        acc[...] = jnp.zeros_like(acc)
+        last_row, last_col = peer_tile(7), col_tile(7)
+
+        def early(t):
+            @pl.when((t // 2 != last_col) & (t != last_row))
             def _():
-                peer_in(p, j - 1)
-
-        def peer_in(q, j):
-            for h in range(2):
-                row_in(q, peer_tile(j), h)
-            unpack_row(q, peer_tile(j))
-
-        loop(0, 8, arrive)
-        acc[...] = jnp.zeros_like(acc)
-        loop(0, 8, lambda j: fold(row_tile(j)))
-        loop(0, 7, lambda j: fold(peer_tile(j)))
-        peer_in(p, 7)
-        fold(peer_tile(7))
-
-        @pl.when(first)
+                fold(t)
+
+        loop(0, TILES, early)
+        peers_open(p, 7, 8)
+
+        @pl.when(last_row // 2 != last_col)
         def _():
-            field_last()
+            fold(last_row)
+
+        for h in range(2):
+            col_in(step, col_tile(7), h)
+        unpack_col(step, col_tile(7))
+        loop(0, 2, lambda i: fold(2 * last_col + i))
+        once(field_last)
 
         scale = jnp.where(first, 1.0, 0.0)
 
@@ -615,33 +582,45 @@
             put(sq, b, value)
 
         def store(u, value):
-            rbuf[p + 1, me, u] = value
+            rbuf[1, me, u] = value
 
         compact(sq, store)
         row_drain(p)
+        for h in range(2):
+            across_copy(p, step, h).wait_send()
 
         acc[...] = jnp.zeros_like(acc)
 
-        def arrive_square(j):
-            for h in range(2):
-
-                @pl.when(j > 0)
-                def _():
-                    row_in(p + 1, row_tile(j), h)
-
-                row_out(p + 1, j, h, start)
-
-            unpack_row(p + 1, row_tile(j))
-            fold(row_tile(j))
-
-            @pl.when(j > 0)
-            def _():
-                peer_in(p + 1, j - 1)
-                fold(peer_tile(j - 1))
-
-        loop(0, 8, arrive_square)
-        peer_in(p + 1, 7)
-        fold(peer_tile(7))
+        def rows_fold(from_, to_):
+            def one(j):
+                unpack_row(p + 1, row_tile(j))
+                fold(row_tile(j))
+
+            loop(from_, to_, one)
+
+        def peers_fold(from_, to_):
+            def one(j):
+                for h in range(2):
+                    row_in(p + 1, peer_tile(j), h)
+                unpack_row(p + 1, peer_tile(j))
+                fold(peer_tile(j))
+
+            loop(from_, to_, one)
+
+        row_pass(p + 1, (0, 0), (0, 1))
+        rows_fold(0, 1)
+        row_pass(p + 1, (2, 0), (3, 0), (1, 0))
+        row_pass(p + 1, (3, 1), (1, 1), (2, 1))
+        peers_fold(0, 1)
+        rows_fold(1, 4)
+        row_pass(p + 1, (6, 0), (4, 0), (6, 1))
+        peers_fold(1, 4)
+        row_pass(p + 1, (4, 1), (5, 1), (5, 0))
+        rows_fold(4, 7)
+        row_pass(p + 1, (7, 1), (7, 0))
+        peers_fold(4, 7)
+        rows_fold(7, 8)
+        peers_fold(7, 8)
 
         for b in range(16):
             at, fi, fj, same = pieces(b)
@@ -649,7 +628,7 @@
             put(cur, b, value)
 
         row_drain(p + 1)
-        col_drain(p, step)
+        col_drain(step)
 
         @pl.when(step + 1 < STEPS)
         def _():
@@ -666,13 +645,14 @@
         out_ref[at] = cur[b] * jnp.where(left, keep_left, keep_right)
 
 
-def body(centers, charge_sites, charges, amplitudes, widths, core_matrix, pattern):
+def run(cap, number, *operands):
+    pairs = cap // 2
     vmem = pl.BlockSpec(memory_space=pltpu.VMEM)
     smem = pl.BlockSpec(memory_space=pltpu.SMEM)
     f32, bf16 = jnp.float32, jnp.bfloat16
     dma = pltpu.SemaphoreType.DMA
-    out, flag = pl.pallas_call(
-        kernel,
+    return pl.pallas_call(
+        functools.partial(kernel, cap),
         out_shape=(
             jax.ShapeDtypeStruct((512, 256), f32),
             jax.ShapeDtypeStruct((1, 1), jnp.int32),
@@ -680,14 +660,14 @@
         in_specs=[smem, smem, smem, vmem, vmem, vmem, vmem],
         out_specs=(vmem, smem),
         scratch_shapes=[
-            pltpu.VMEM((4, TILES, PAIRS, BLOCK, 128), f32),
-            pltpu.VMEM((2, ROWS, PAIRS, BLOCK, 128), f32),
+            pltpu.VMEM((2, TILES, pairs, BLOCK, 128), f32),
+            pltpu.VMEM((2, ROWS, pairs, BLOCK, 128), f32),
             pltpu.VMEM((TILES, 512, 256), bf16),
             pltpu.VMEM((TILES, 512, 256), bf16),
             pltpu.VMEM((TILES, 256, 256), bf16),
             pltpu.VMEM((TILES, 256, 256), bf16),
             pltpu.VMEM((512, 256), f32),
-            pltpu.VMEM((2 * PAIRS + 2, BLOCK, 128), f32),
+            pltpu.VMEM((2 * pairs + 2, BLOCK, 128), f32),
             pltpu.VMEM((32, BLOCK, 128), f32),
             pltpu.VMEM((32, BLOCK, 128), f32),
             pltpu.VMEM((4, 512, 128), f32),
@@ -724,9 +704,13 @@
             dma((2,)),
         ],
         compiler_params=pltpu.CompilerParams(
-            collective_id=0, has_side_effects=True, vmem_limit_bytes=58 * 1024 * 1024
+            collective_id=number, has_side_effects=True, vmem_limit_bytes=58 * 1024 * 1024
         ),
-    )(
+    )(*operands)
+
+
+def body(centers, charge_sites, charges, amplitudes, widths, core_matrix, pattern):
+    operands = (
         pattern,
         amplitudes,
         widths,
@@ -735,13 +719,8 @@
         charges[None, :],
         core_matrix,
     )
-    return lax.cond(
-        flag[0, 0] > CAP,
-        lambda: dense_body(
-            centers, charge_sites, charges, amplitudes, widths, core_matrix, pattern
-        ),
-        lambda: out,
-    )
+    out, flag = run(CAP, 0, *operands)
+    return lax.cond(flag[0, 0] > CAP, lambda: run(FULL, 1, *operands)[0], lambda: out)
 
 
 def solution(mesh):

time: 161 us -> 131 us (0.81)
  Pallas kernels: 144 us -> 127 us
  between operations: 14 us -> 0.7 us
    pallas_call x1, Pallas kernels: 144 us -> 127 us  [run(): pl.pallas_call(functools.partial(kernel, cap), out_shape=(jax.ShapeDtypeS...]
where the time goes in v3:
time: 131 us; the launch traced here: 130 us
  Pallas kernels  127 us (97%)
  local copies, waits for them, and re-layouts  2.79 us (2%)
    pallas_call x1, Pallas kernels, run(): pl.pallas_call(functools.partial(kernel, cap), out_shape=(jax.ShapeDtypeS...  127 us
    unnamed x16, local copies, waits for them, and re-layouts  2.79 us

profile of v3, /device:TPU:1, one launch (start us, length us, event | category | flops | bytes accessed | tf_op | source)
XLA Modules:
  0.0 130.0 jit_solution(1721184857377517037)
XLA Ops:
  0.0 0.0 copy-start.4
  0.0 0.0 copy-start
  0.0 0.7 copy-done.4
  0.7 0.7 copy.10.keep_ref
  1.4 0.0 copy-start.1
  1.4 0.0 copy-start.2
  1.4 126.5 %shard_map.75 = (f32[512,256]{1,0:T(8,128)S(1)}, s32[1,1]{1,0:T(1,128)}) custom-call(s32[8,4]{1,0:T(8,128)} %copy.10.keep_ref, f32[6]{0:T(128)} %amp_ref.1, f32[6]{0:T(128)} %width_ref.1, f32[3,4096]{1,0:T(4,128)} %centers_ref.1, f32[3,512]{1,0:T(4,128)} %sites_ref.1, f32[1,512]{1,0:T(1,128)} %bitcast.2, f32[512,256]{1,0:T(8,128)} %core_ref.1), custom_call_target="tpu_custom_call" | custom-call | tf_op jit(solution)/shard_map/pallas_call | solution.py:654
  128.5 0.0 copy-start.3
  128.5 0.0 copy-start.5
  128.5 0.0 copy-start.6
  128.6 0.0 copy-done
  128.6 0.0 copy-done.1
  128.6 0.0 copy-done.2
  128.6 0.6 copy-done.3
  129.2 0.0 copy-done.5
  129.2 0.0 copy-done.6
  129.2 0.8 copy.15
  (1 shorter events, 0.0 us)
Async XLA Ops:
  0.0 0.7 copy-start.4
  0.0 128.6 %copy-start = (f32[512,256]{1,0:T(8,128)S(1)}, f32[512,256]{1,0:T(8,128)}, u32[]{:S(2)}) copy-start(f32[512,256]{1,0:T(8,128)} %core_ref.1) | copy-start | bytes 1572868
  1.4 127.2 %copy-start.1 = (f32[3,4096]{1,0:T(4,128)S(1)}, f32[3,4096]{1,0:T(4,128)}, u32[]{:S(2)}) copy-start(f32[3,4096]{1,0:T(4,128)} %centers_ref.1) | copy-start | bytes 147460
  1.4 127.2 %copy-start.2 = (f32[3,512]{1,0:T(4,128)S(1)}, f32[3,512]{1,0:T(4,128)}, u32[]{:S(2)}) copy-start(f32[3,512]{1,0:T(4,128)} %sites_ref.1) | copy-start | bytes 18436
  128.5 0.7 copy-start.3
  128.5 0.7 copy-start.5
  128.5 0.7 copy-start.6

commit v4 on v3

--- a/solution.py
+++ b/solution.py
@@ -11,7 +11,7 @@
 STEPS = 2
 ROWS, COLS, SECS = 8, 8, 2
 TILES = COLS * SECS
-CAP = 20
+CAP = 16
 FULL = 32
 CHUNK = 128
 LOG2E = 1.4426950408889634
@@ -32,6 +32,9 @@
     flag_ref,
     rbuf,
     cbuf,
+    xbuf,
+    over_out,
+    over_in,
     a_hi,
     a_lo,
     b_hi,
@@ -61,6 +64,10 @@
     r_recv,
     c_send,
     c_recv,
+    x_send,
+    x_recv,
+    o_send,
+    o_recv,
     hr_send,
     hr_recv,
     hc_send,
@@ -116,19 +123,24 @@
 
     lane1 = lax.broadcasted_iota(jnp.int32, (1, 128), 1)
     before = 0
-    codes = jnp.full((1, 128), pairs, jnp.int32)
+    empty = 2 * pairs
+    codes = jnp.full((1, 128), empty, jnp.int32)
     blocks = jnp.zeros((1, 128), jnp.int32)
     for b in range(32):
         keep = keep_ref[b // 4, b % 4]
         turned = (before + b) % 2
-        there = before // 2 + (pairs + 1) * turned
-        code = jnp.where((keep == 1) & (before < cap), there, pairs)
+        spare = 2 * cap - 1 - before
+        own = core * pairs + before // 2 + (2 * pairs + 1) * turned
+        other = (1 - core) * pairs + spare // 2 + (2 * pairs + 1) * (1 - turned)
+        code = jnp.where(before < cap, own, jnp.where(spare >= cap // 2, other, empty))
+        code = jnp.where(keep == 1, code, empty)
         codes = jnp.where(lane1 == b, code, codes)
-        at = jnp.where(keep == 1, before, 127)
-        blocks = jnp.where(lane1 == at, b // 2 + 16 * turned, blocks)
+        at = jnp.where(before < cap, before, jnp.where(spare >= cap // 2, 64 + spare, 127))
+        at = jnp.where(keep == 1, at, 127)
+        blocks = jnp.where(lane1 == at, b // 2 + 16 * ((at + b) % 2), blocks)
         before = before + keep
     hdr_ref[...] = jnp.where(lane1 == 127, before, codes)
-    inv_line[...] = jnp.where(lane1 < cap, blocks, 0)
+    inv_line[...] = jnp.where(lane1 < 127, blocks, 0)
     scale_line = jnp.zeros((1, 128), jnp.float32)
     for g in range(6):
         wide = jnp.full((1, 128), width_ref[g], jnp.float32)
@@ -144,16 +156,38 @@
         dst[number] = value
         dst[16 + number] = pltpu.roll(value, BLOCK, 1)
 
-    def compact(src, store):
-        for u in range(pairs):
-            value = jnp.where(left, src[inv_ref[0, 2 * u]], src[inv_ref[0, 2 * u + 1]])
-            store(u, value)
-
-    def unpack(load, table, tile, store):
-        for u in range(pairs):
-            value = load(u)
-            work[u] = value
-            work[pairs + 1 + u] = pltpu.roll(value, BLOCK, 1)
+    def pair(src, first_slot):
+        return jnp.where(left, src[inv_ref[0, first_slot]], src[inv_ref[0, first_slot + 1]])
+
+    def over_copy(q):
+        return pltpu.make_async_remote_copy(
+            src_ref=over_out.at[q],
+            dst_ref=over_in.at[q],
+            send_sem=o_send.at[q],
+            recv_sem=o_recv.at[q],
+            device_id=sibling,
+            device_id_type=MESH,
+        )
+
+    def spill(src, q):
+        for u in range(half):
+            over_out[q, u] = pair(src, 64 + 2 * (half + u))
+
+    def compact_first(src, store):
+        for u in range(half):
+            store(u, pair(src, 2 * u))
+
+    def compact_second(src, q, store):
+        over_copy(q).wait()
+        for u in range(half, pairs):
+            slot = 2 * u + jnp.where(left, 0, 1)
+            store(u, jnp.where(slot < before, pair(src, 2 * u), over_in[q, u - half]))
+
+    def lay(number, value):
+        work[number] = value
+        work[2 * pairs + 1 + number] = pltpu.roll(value, BLOCK, 1)
+
+    def unpack(table, tile, store):
         for b in range(16):
             value = jnp.where(
                 left, work[table[tile, 0, 2 * b]], work[table[tile, 0, 2 * b + 1]]
@@ -162,15 +196,30 @@
             low = (value - high.astype(jnp.float32)).astype(jnp.bfloat16)
             store(b, high, low)
 
-    def unpack_row(p, tile):
-        def store(b, high, low):
-            at = (tile, pl.ds((b // 2) * BLOCK, BLOCK), pl.ds((b % 2) * 128, 128))
-            a_hi[at] = high
-            a_lo[at] = low
-
-        unpack(lambda u: rbuf[p % 2, tile, u], trow, tile, store)
-
-    def unpack_col(step, tile):
+    def unpack_chip(q, tile):
+        for u in range(pairs):
+            lay(u, rbuf[q, tile, u])
+            lay(pairs + u, rbuf[q, tile + 2, u])
+
+        def one(i, c):
+            at_tile = tile + 2 * i
+
+            def store(b, high, low):
+                at = (at_tile, pl.ds((b // 2) * BLOCK, BLOCK), pl.ds((b % 2) * 128, 128))
+                a_hi[at] = high
+                a_lo[at] = low
+
+            unpack(trow, at_tile, store)
+            return c
+
+        lax.fori_loop(0, 2, one, 0)
+
+    def unpack_col(s, tile):
+        for u in range(pairs):
+            lay(core * pairs + u, cbuf[s, tile, u])
+        for u in range(half):
+            lay((1 - core) * pairs + half + u, xbuf[s, tile, u])
+
         def store(b, high, low):
             at = (
                 2 * tile + b // 8,
@@ -180,14 +229,16 @@
             b_hi[at] = high
             b_lo[at] = low
 
-        unpack(lambda u: cbuf[step, tile, u], tcol, tile, store)
-
-    def fold(tile):
+        unpack(tcol, tile, store)
+
+    def fold(*tiles):
         dot = functools.partial(jnp.dot, preferred_element_type=jnp.float32)
-        total = dot(a_hi[tile], b_hi[tile])
-        total = total + dot(a_lo[tile], b_hi[tile])
-        total = total + dot(a_hi[tile], b_lo[tile])
-        acc[...] += total
+        total = acc[...]
+        for tile in tiles:
+            total = total + dot(a_hi[tile], b_hi[tile])
+            total = total + dot(a_lo[tile], b_hi[tile])
+            total = total + dot(a_hi[tile], b_lo[tile])
+        acc[...] = total
 
 
     def row_copy(p, tile, j, kind, h, dev):
@@ -222,11 +273,14 @@
     def swap(j):
         return mid(j) * (j // 2 - 1) + (1 - mid(j)) * (j % 2)
 
+    def chip_tile(j):
+        return 4 * ((z + hop(j)) % 4) + (sec + swap(j)) % 2
+
     def row_tile(j):
-        return 4 * ((z + hop(j)) % 4) + 2 * core + (sec + swap(j)) % 2
+        return chip_tile(j) + 2 * core
 
     def peer_tile(j):
-        return 4 * ((z + hop(j)) % 4) + 2 * (1 - core) + (sec + swap(j)) % 2
+        return chip_tile(j) + 2 * (1 - core)
 
     def col_tile(j):
         return 4 * ((hi + swap(j)) % 2) + (y + hop(j)) % 4
@@ -239,6 +293,17 @@
             send_sem=c_send.at[0, 2, h],
             recv_sem=c_recv.at[s, row, h],
             device_id=across,
+            device_id_type=MESH,
+        )
+
+    def x_copy(s, j):
+        tile = col_tile(j)
+        return pltpu.make_async_remote_copy(
+            src_ref=cbuf.at[s, tile, pl.ds(half, half)],
+            dst_ref=xbuf.at[s, tile],
+            send_sem=x_send.at[j],
+            recv_sem=x_recv.at[s, tile],
+            device_id=sibling,
             device_id_type=MESH,
         )
 
@@ -266,9 +331,17 @@
         (1, 0): (0, 1),
         (1, 1): (0, 1),
         (2, 0): (0,),
+        (2, 1): (),
+        (3, 0): (),
         (3, 1): (1,),
         (4, 0): (0,),
+        (4, 1): (),
+        (5, 0): (),
         (5, 1): (1,),
+        (6, 0): (),
+        (6, 1): (),
+        (7, 0): (),
+        (7, 1): (),
     }
     row_to = (sibling, z_up, z_down, x_peer)
     col_to = (y_up, y_down)
@@ -301,6 +374,8 @@
                 col_in(s, col_tile(j), h)
             for kind in col_plan[j, h]:
                 col_act(s, j, h, kind, start)
+            if h == 1:
+                x_copy(s, j).start()
 
     def drain(copy):
         copy.wait_send()
@@ -320,6 +395,8 @@
         for (j, h), kinds in col_plan.items():
             for kind in kinds:
                 col_act(s, j, h, kind, drain)
+            if h == 1:
+                x_copy(s, j).wait_send()
 
     def small(src, dst, send, recv, dev):
         return pltpu.make_async_remote_copy(
@@ -338,29 +415,29 @@
     for b in range(16):
         put(cur, b, core_ref[pl.ds((b // 2) * BLOCK, BLOCK), pl.ds((b % 2) * 128, 128)])
 
-    def keep_iterate(p, s):
+    def keep_iterate(s):
         def store(u, value):
-            rbuf[p % 2, me, u] = value
+            rbuf[0, me, u] = value
             cbuf[s, row, u] = value
 
-        compact(cur, store)
+        return store
 
     inv_copy.wait()
     coef_copy.wait()
-    keep_iterate(0, 0)
-    work[pairs] = jnp.zeros((BLOCK, 128), jnp.float32)
-    work[2 * pairs + 1] = jnp.zeros((BLOCK, 128), jnp.float32)
+    spill(cur, 0)
+    compact_first(cur, keep_iterate(0))
+    work[empty] = jnp.zeros((BLOCK, 128), jnp.float32)
+    work[4 * pairs + 1] = jnp.zeros((BLOCK, 128), jnp.float32)
     hrow[me] = hdr_ref[...]
     hcol[row] = hdr_ref[...]
 
-    pl.semaphore_wait(barrier, TILES + ROWS - 1)
-
     def hr_copy(d):
         return small(hdr_ref, hrow.at[me], hr_send.at[d], hr_recv.at[me], row_mate(d))
 
     def hc_copy(d):
         return small(hdr_ref, hcol.at[row], hc_send.at[d], hc_recv.at[row], col_mate(d))
 
+    pl.semaphore_wait(barrier, TILES + ROWS - 1)
     loop(1, TILES, lambda d: hr_copy(d).start())
     loop(1, ROWS, lambda d: hc_copy(d).start())
 
@@ -456,11 +533,13 @@
     def field_third():
         loop(1, TILES, f2_wait)
         total = f_two[0]
-        most = f_two[0]
         for c in range(1, TILES):
-            value = f_two[c]
-            total = total + value
-            most = jnp.maximum(most, value)
+            total = total + f_two[c]
+        most = jnp.zeros((8, 128), jnp.float32)
+        for c in range(TILES):
+            most = jnp.maximum(most, f_two[c] + cap // 2)
+            if c % 4 < 2:
+                most = jnp.maximum(most, f_two[c] + f_two[c + 2])
         total = jnp.where(line8 < 4, total, most)
         f_all[...] = total
         f_three[row] = total
@@ -486,14 +565,21 @@
         p = 2 * step
         first = step == 0
 
-        def rows_open(q, from_, to_):
-            loop(from_, to_, lambda j: unpack_row(q, row_tile(j)))
-
-        def peers_open(q, from_, to_):
+        def chips_open(q, from_, to_):
             def one(j):
                 for h in range(2):
                     row_in(q, peer_tile(j), h)
-                unpack_row(q, peer_tile(j))
+                unpack_chip(q % 2, chip_tile(j))
+
+            loop(from_, to_, one)
+
+        def cols_open(from_, to_):
+            def one(j):
+                tile = col_tile(j)
+                small(
+                    xbuf.at[step, tile], xbuf.at[step, tile], x_send.at[0], x_recv.at[step, tile], sibling
+                ).wait_recv()
+                unpack_col(step, tile)
 
             loop(from_, to_, one)
 
@@ -506,65 +592,62 @@
         def chunks(from_, to_):
             return lambda: loop(from_, to_, field_chunk)
 
-        for h in range(2):
-            row_pass(p, (0, h))
-            col_pass(step, (0, h))
+        over_copy(0).start()
+        row_pass(p, (0, 0))
+        col_pass(step, (0, 0))
+        compact_second(cur, 0, keep_iterate(step))
+        row_pass(p, (0, 1))
+        col_pass(step, (0, 1))
         once(spread_sites, chunks(0, 9), read_tables)
-        rows_open(p, 0, 1)
-        unpack_col(step, col_tile(0))
-        col_pass(step, (2, 0))
+        chips_open(p, 0, 1)
+        cols_open(0, 1)
+        col_pass(step, (2, 0), (3, 0))
         row_pass(p, (2, 0), (3, 0), (1, 0))
         across_copy(p, step, 0).start()
         once(chunks(9, 18))
         row_pass(p, (3, 1), (1, 1))
         across_copy(p, step, 1).start()
-        col_pass(step, (3, 1))
+        col_pass(step, (3, 1), (2, 1))
         row_pass(p, (2, 1))
         once(chunks(18, 26))
-        rows_open(p, 1, 4)
+        chips_open(p, 1, 3)
         col_pass(step, (1, 0))
         row_pass(p, (6, 0))
         col_pass(step, (1, 1))
         once(chunks(26, 32), field_first)
-        unpack_col(step, col_tile(1))
+        chips_open(p, 3, 4)
         row_pass(p, (4, 0), (6, 1), (4, 1))
-        peers_open(p, 0, 3)
+        cols_open(1, 4)
         row_pass(p, (5, 1), (5, 0))
-        col_in(step, col_tile(2), 1)
-        col_in(step, col_tile(3), 0)
-        loop(2, 4, lambda j: unpack_col(step, col_tile(j)))
-        col_pass(step, (4, 0), (5, 1))
+        col_pass(step, (4, 0), (5, 0), (5, 1), (4, 1))
         once(field_second)
-        rows_open(p, 4, 7)
+        chips_open(p, 4, 7)
         row_pass(p, (7, 0), (7, 1))
-        peers_open(p, 3, 6)
-        rows_open(p, 7, 8)
-        col_in(step, col_tile(4), 1)
-        col_in(step, col_tile(5), 0)
-        for h in range(2):
-            col_in(step, col_tile(6), h)
-        loop(4, 7, lambda j: unpack_col(step, col_tile(j)))
+        col_pass(step, (6, 0), (6, 1))
+        cols_open(4, 7)
         once(field_third)
-        peers_open(p, 6, 7)
         acc[...] = jnp.zeros_like(acc)
-        last_row, last_col = peer_tile(7), col_tile(7)
-
-        def early(t):
-            @pl.when((t // 2 != last_col) & (t != last_row))
+        last_z, last_col = chip_tile(7) // 4, col_tile(7)
+
+        def early(r):
+            @pl.when((r // 2 != last_z) & (r != last_col))
             def _():
-                fold(t)
-
-        loop(0, TILES, early)
-        peers_open(p, 7, 8)
-
-        @pl.when(last_row // 2 != last_col)
-        def _():
-            fold(last_row)
-
-        for h in range(2):
-            col_in(step, col_tile(7), h)
-        unpack_col(step, col_tile(7))
-        loop(0, 2, lambda i: fold(2 * last_col + i))
+                fold(2 * r, 2 * r + 1)
+
+        loop(0, ROWS, early)
+        chips_open(p, 7, 8)
+        col_pass(step, (7, 0), (7, 1))
+
+        def late(i):
+            r = 2 * last_z + i
+
+            @pl.when(r != last_col)
+            def _():
+                fold(2 * r, 2 * r + 1)
+
+        loop(0, 2, late)
+        cols_open(7, 8)
+        fold(2 * last_col, 2 * last_col + 1)
         once(field_last)
 
         scale = jnp.where(first, 1.0, 0.0)
@@ -584,43 +667,36 @@
         def store(u, value):
             rbuf[1, me, u] = value
 
-        compact(sq, store)
+        spill(sq, 1)
+        over_copy(1).start()
+        compact_first(sq, store)
         row_drain(p)
         for h in range(2):
             across_copy(p, step, h).wait_send()
 
-        acc[...] = jnp.zeros_like(acc)
-
-        def rows_fold(from_, to_):
-            def one(j):
-                unpack_row(p + 1, row_tile(j))
-                fold(row_tile(j))
-
-            loop(from_, to_, one)
-
-        def peers_fold(from_, to_):
+        def chips_fold(from_, to_):
             def one(j):
                 for h in range(2):
                     row_in(p + 1, peer_tile(j), h)
-                unpack_row(p + 1, peer_tile(j))
-                fold(peer_tile(j))
+                tile = chip_tile(j)
+                unpack_chip(1, tile)
+                fold(tile, tile + 2)
 
             loop(from_, to_, one)
 
-        row_pass(p + 1, (0, 0), (0, 1))
-        rows_fold(0, 1)
+        row_pass(p + 1, (0, 0))
+        compact_second(sq, 1, store)
+        row_pass(p + 1, (0, 1))
+        acc[...] = jnp.zeros_like(acc)
+        chips_fold(0, 1)
         row_pass(p + 1, (2, 0), (3, 0), (1, 0))
         row_pass(p + 1, (3, 1), (1, 1), (2, 1))
-        peers_fold(0, 1)
-        rows_fold(1, 4)
+        chips_fold(1, 4)
         row_pass(p + 1, (6, 0), (4, 0), (6, 1))
-        peers_fold(1, 4)
         row_pass(p + 1, (4, 1), (5, 1), (5, 0))
-        rows_fold(4, 7)
+        chips_fold(4, 7)
         row_pass(p + 1, (7, 1), (7, 0))
-        peers_fold(4, 7)
-        rows_fold(7, 8)
-        peers_fold(7, 8)
+        chips_fold(7, 8)
 
         for b in range(16):
             at, fi, fj, same = pieces(b)
@@ -632,7 +708,9 @@
 
         @pl.when(step + 1 < STEPS)
         def _():
-            keep_iterate(p + 2, step + 1)
+            spill(cur, 0)
+            compact_first(cur, keep_iterate(step + 1))
+
 
         return carry
 
@@ -662,12 +740,15 @@
         scratch_shapes=[
             pltpu.VMEM((2, TILES, pairs, BLOCK, 128), f32),
             pltpu.VMEM((2, ROWS, pairs, BLOCK, 128), f32),
+            pltpu.VMEM((2, ROWS, pairs // 2, BLOCK, 128), f32),
+            pltpu.VMEM((2, pairs // 2, BLOCK, 128), f32),
+            pltpu.VMEM((2, pairs // 2, BLOCK, 128), f32),
             pltpu.VMEM((TILES, 512, 256), bf16),
             pltpu.VMEM((TILES, 512, 256), bf16),
             pltpu.VMEM((TILES, 256, 256), bf16),
             pltpu.VMEM((TILES, 256, 256), bf16),
             pltpu.VMEM((512, 256), f32),
-            pltpu.VMEM((2 * pairs + 2, BLOCK, 128), f32),
+            pltpu.VMEM((4 * pairs + 2, BLOCK, 128), f32),
             pltpu.VMEM((32, BLOCK, 128), f32),
             pltpu.VMEM((32, BLOCK, 128), f32),
             pltpu.VMEM((4, 512, 128), f32),
@@ -691,6 +772,10 @@
             dma((4, TILES, 2)),
             dma((8, 3, 2)),
             dma((2, ROWS, 2)),
+            dma((ROWS,)),
+            dma((2, ROWS)),
+            dma((2,)),
+            dma((2,)),
             dma((TILES,)),
             dma((TILES,)),
             dma((ROWS,)),
@@ -720,7 +805,7 @@
         core_matrix,
     )
     out, flag = run(CAP, 0, *operands)
-    return lax.cond(flag[0, 0] > CAP, lambda: run(FULL, 1, *operands)[0], lambda: out)
+    return lax.cond(flag[0, 0] > 2 * CAP, lambda: run(FULL, 1, *operands)[0], lambda: out)
 
 
 def solution(mesh):

time: 131 us -> 122 us (0.931)
  Pallas kernels: 127 us -> 119 us
    pallas_call x1, Pallas kernels: 127 us -> 119 us  [run(): pl.pallas_call(functools.partial(kernel, cap), out_shape=(jax.ShapeDtypeS...]
where the time goes in v4:
time: 122 us
  Pallas kernels  119 us (98%)
  local copies, waits for them, and re-layouts  2.79 us (2%)
    pallas_call x1, Pallas kernels, run(): pl.pallas_call(functools.partial(kernel, cap), out_shape=(jax.ShapeDtypeS...  119 us
    unnamed x16, local copies, waits for them, and re-layouts  2.79 us

profile of v4, /device:TPU:1, one launch (start us, length us, event | category | flops | bytes accessed | tf_op | source)
XLA Modules:
  0.0 122.2 jit_solution(15050234005609874677)
XLA Ops:
  0.0 0.0 copy-start.4
  0.0 0.0 copy-start
  0.0 0.7 copy-done.4
  0.7 0.7 copy.10.keep_ref
  1.4 0.0 copy-start.1
  1.4 0.0 copy-start.2
  1.4 118.7 %shard_map.75 = (f32[512,256]{1,0:T(8,128)S(1)}, s32[1,1]{1,0:T(1,128)}) custom-call(s32[8,4]{1,0:T(8,128)} %copy.10.keep_ref, f32[6]{0:T(128)} %amp_ref.1, f32[6]{0:T(128)} %width_ref.1, f32[3,4096]{1,0:T(4,128)} %centers_ref.1, f32[3,512]{1,0:T(4,128)} %sites_ref.1, f32[1,512]{1,0:T(1,128)} %bitcast.2, f32[512,256]{1,0:T(8,128)} %core_ref.1), custom_call_target="tpu_custom_call" | custom-call | tf_op jit(solution)/shard_map/pallas_call | solution.py:732
  120.7 0.0 copy-start.3
  120.7 0.0 copy-start.5
  120.7 0.0 copy-start.6
  120.8 0.0 copy-done
  120.8 0.0 copy-done.1
  120.8 0.0 copy-done.2
  120.8 0.6 copy-done.3
  121.4 0.0 copy-done.5
  121.4 0.0 copy-done.6
  121.4 0.8 copy.15
  (1 shorter events, 0.0 us)
Async XLA Ops:
  0.0 0.7 copy-start.4
  0.0 120.8 %copy-start = (f32[512,256]{1,0:T(8,128)S(1)}, f32[512,256]{1,0:T(8,128)}, u32[]{:S(2)}) copy-start(f32[512,256]{1,0:T(8,128)} %core_ref.1) | copy-start | bytes 1572868
  1.4 119.4 %copy-start.1 = (f32[3,4096]{1,0:T(4,128)S(1)}, f32[3,4096]{1,0:T(4,128)}, u32[]{:S(2)}) copy-start(f32[3,4096]{1,0:T(4,128)} %centers_ref.1) | copy-start | bytes 147460
  1.4 119.4 %copy-start.2 = (f32[3,512]{1,0:T(4,128)S(1)}, f32[3,512]{1,0:T(4,128)}, u32[]{:S(2)}) copy-start(f32[3,512]{1,0:T(4,128)} %sites_ref.1) | copy-start | bytes 18436
  120.7 0.7 copy-start.3
  120.7 0.7 copy-start.5
  120.7 0.7 copy-start.6

commit v5 on v4

--- a/solution.py
+++ b/solution.py
@@ -431,13 +431,21 @@
     hrow[me] = hdr_ref[...]
     hcol[row] = hdr_ref[...]
 
+    def f1_copy(d):
+        return small(f_one.at[row], f_one.at[row], f1_send.at[d], f1_recv.at[row], col_mate(d))
+
     def hr_copy(d):
         return small(hdr_ref, hrow.at[me], hr_send.at[d], hr_recv.at[me], row_mate(d))
 
     def hc_copy(d):
         return small(hdr_ref, hcol.at[row], hc_send.at[d], hc_recv.at[row], col_mate(d))
 
+    for c in range(4):
+        for a in range(3):
+            f_one[row, 4 * a + c : 4 * a + c + 1, :] = sites_ref[a : a + 1, c * 128 : (c + 1) * 128]
+        f_one[row, 12 + c : 13 + c, :] = charges_ref[0:1, c * 128 : (c + 1) * 128]
     pl.semaphore_wait(barrier, TILES + ROWS - 1)
+    loop(1, ROWS, lambda d: f1_copy(d).start())
     loop(1, TILES, lambda d: hr_copy(d).start())
     loop(1, ROWS, lambda d: hc_copy(d).start())
 
@@ -460,24 +468,23 @@
         two.wait()
 
 
-    def spread_sites():
-        for a in range(4):
+    def spread_centers():
+        for a in range(3):
             for c in range(4):
-                if a < 3:
-                    line = sites_ref[a : a + 1, c * 128 : (c + 1) * 128]
-                else:
-                    line = charges_ref[0:1, c * 128 : (c + 1) * 128]
+                at = pl.ds(pl.multiple_of(row * 512 + c * 128, 128), 128)
                 fan[a, c * 128 : (c + 1) * 128, :] = jnp.transpose(
-                    jnp.broadcast_to(line, (128, 128))
+                    jnp.broadcast_to(centers_ref[a : a + 1, at], (128, 128))
                 )
+        f_own[...] = jnp.zeros_like(f_own)
 
     def field_chunk(ch):
-        at = pl.ds(pl.multiple_of(ch * CHUNK, CHUNK), CHUNK)
-        px = centers_ref[0:1, at]
-        py = centers_ref[1:2, at]
-        pz = centers_ref[2:3, at]
-
-        def some(m, total):
+        mate, c = (row + ch // 4) % ROWS, ch % 4
+        px = f_one[mate, pl.ds(c, 1), :]
+        py = f_one[mate, pl.ds(4 + c, 1), :]
+        pz = f_one[mate, pl.ds(8 + c, 1), :]
+        charge = f_one[mate, pl.ds(12 + c, 1), :]
+
+        def some(m, carry):
             part = pl.ds(m * 32, 32)
             dx = fan[0, part, :] - px
             dy = fan[1, part, :] - py
@@ -486,18 +493,14 @@
             value = amp_ref[0] * jnp.exp2(distance * coef_ref[0, 0])
             for g in range(1, 6):
                 value = value + amp_ref[g] * jnp.exp2(distance * coef_ref[0, g])
-            return total + value * fan[3, part, :]
-
-        total = lax.fori_loop(0, 16, some, jnp.zeros((32, 128), jnp.float32), unroll=4)
-        f_own[ch // 4, pl.ds(ch % 4, 1), :] = jnp.sum(total, axis=0, keepdims=True)
-
-    def f1_copy(d):
-        other = (row + d) % ROWS
-        return small(f_own.at[other], f_one.at[row], f1_send.at[d], f1_recv.at[row], col_mate(d))
+            f_own[part, :] += value * charge
+            return carry
+
+        lax.fori_loop(0, 16, some, 0, unroll=4)
 
     def f1_wait(d):
         other = (row + d) % ROWS
-        small(f_own.at[row], f_one.at[other], f1_send.at[d], f1_recv.at[other], col_mate(d)).wait_recv()
+        small(f_one.at[other], f_one.at[other], f1_send.at[d], f1_recv.at[other], col_mate(d)).wait_recv()
 
     def f2_copy(d):
         return small(f_sum, f_two.at[me], f2_send.at[d], f2_recv.at[me], row_mate(d))
@@ -515,15 +518,15 @@
 
     line8 = lax.broadcasted_iota(jnp.int32, (8, 128), 0)
 
-    def field_first():
-        f_one[row] = f_own[row]
-        loop(1, ROWS, lambda d: f1_copy(d).start())
+    def charges_in():
+        loop(1, ROWS, f1_wait)
 
     def field_second():
-        loop(1, ROWS, f1_wait)
-        total = f_one[0]
-        for r in range(1, ROWS):
-            total = total + f_one[r]
+        lines = [
+            jnp.sum(jnp.transpose(f_own[c * 128 : (c + 1) * 128, :]), axis=0, keepdims=True)
+            for c in range(4)
+        ]
+        total = jnp.concatenate(lines + lines, axis=0)
         count = jnp.broadcast_to(hdr_ref[...], (8, 128)).astype(jnp.float32)
         total = jnp.where(line8 < 4, total, count)
         f_sum[...] = total
@@ -598,34 +601,39 @@
         compact_second(cur, 0, keep_iterate(step))
         row_pass(p, (0, 1))
         col_pass(step, (0, 1))
-        once(spread_sites, chunks(0, 9), read_tables)
+        acc[...] = jnp.zeros_like(acc)
+        once(spread_centers, chunks(0, 4), charges_in, chunks(4, 8))
+        row_pass(p, (1, 0))
+        across_copy(p, step, 0).start()
+        col_pass(step, (2, 0))
+        row_pass(p, (2, 0), (3, 0))
+        once(read_tables, chunks(8, 12))
         chips_open(p, 0, 1)
+        row_pass(p, (1, 1))
+        across_copy(p, step, 1).start()
+        col_pass(step, (3, 1))
+        row_pass(p, (3, 1), (2, 1))
+        col_pass(step, (2, 1), (3, 0))
+        once(chunks(12, 15))
+        col_pass(step, (1, 0))
         cols_open(0, 1)
-        col_pass(step, (2, 0), (3, 0))
-        row_pass(p, (2, 0), (3, 0), (1, 0))
-        across_copy(p, step, 0).start()
-        once(chunks(9, 18))
-        row_pass(p, (3, 1), (1, 1))
-        across_copy(p, step, 1).start()
-        col_pass(step, (3, 1), (2, 1))
-        row_pass(p, (2, 1))
-        once(chunks(18, 26))
-        chips_open(p, 1, 3)
-        col_pass(step, (1, 0))
+        once(chunks(15, 20))
+        chips_open(p, 1, 2)
         row_pass(p, (6, 0))
         col_pass(step, (1, 1))
-        once(chunks(26, 32), field_first)
-        chips_open(p, 3, 4)
-        row_pass(p, (4, 0), (6, 1), (4, 1))
+        once(chunks(20, 26))
+        row_pass(p, (4, 1), (5, 1), (6, 1), (4, 0), (5, 0))
+        col_pass(step, (4, 0))
+        once(chunks(26, 32), field_second)
+        chips_open(p, 2, 4)
         cols_open(1, 4)
-        row_pass(p, (5, 1), (5, 0))
-        col_pass(step, (4, 0), (5, 0), (5, 1), (4, 1))
-        once(field_second)
-        chips_open(p, 4, 7)
-        row_pass(p, (7, 0), (7, 1))
+        col_pass(step, (5, 0), (5, 1), (4, 1))
+        chips_open(p, 4, 6)
+        once(field_third)
+        row_pass(p, (7, 1), (7, 0))
+        chips_open(p, 6, 7)
         col_pass(step, (6, 0), (6, 1))
         cols_open(4, 7)
-        once(field_third)
         acc[...] = jnp.zeros_like(acc)
         last_z, last_col = chip_tile(7) // 4, col_tile(7)
 
@@ -688,14 +696,16 @@
         compact_second(sq, 1, store)
         row_pass(p + 1, (0, 1))
         acc[...] = jnp.zeros_like(acc)
+        row_pass(p + 1, (2, 0), (3, 0), (1, 0))
         chips_fold(0, 1)
-        row_pass(p + 1, (2, 0), (3, 0), (1, 0))
-        row_pass(p + 1, (3, 1), (1, 1), (2, 1))
-        chips_fold(1, 4)
-        row_pass(p + 1, (6, 0), (4, 0), (6, 1))
-        row_pass(p + 1, (4, 1), (5, 1), (5, 0))
-        chips_fold(4, 7)
+        row_pass(p + 1, (1, 1), (3, 1), (2, 1))
+        chips_fold(1, 2)
+        row_pass(p + 1, (6, 0))
+        chips_fold(2, 3)
+        row_pass(p + 1, (4, 1), (5, 1), (6, 1), (4, 0), (5, 0))
+        chips_fold(3, 5)
         row_pass(p + 1, (7, 1), (7, 0))
+        chips_fold(5, 7)
         chips_fold(7, 8)
 
         for b in range(16):
@@ -751,9 +761,9 @@
             pltpu.VMEM((4 * pairs + 2, BLOCK, 128), f32),
             pltpu.VMEM((32, BLOCK, 128), f32),
             pltpu.VMEM((32, BLOCK, 128), f32),
-            pltpu.VMEM((4, 512, 128), f32),
-            pltpu.VMEM((ROWS, 8, 128), f32),
-            pltpu.VMEM((ROWS, 8, 128), f32),
+            pltpu.VMEM((3, 512, 128), f32),
+            pltpu.VMEM((512, 128), f32),
+            pltpu.VMEM((ROWS, 16, 128), f32),
             pltpu.VMEM((TILES, 8, 128), f32),
             pltpu.VMEM((ROWS, 8, 128), f32),
             pltpu.VMEM((8, 128), f32),

time: 122 us -> 120 us (0.984)
  Pallas kernels: 119 us -> 116 us
    pallas_call x1, Pallas kernels: 119 us -> 116 us  [run(): pl.pallas_call(functools.partial(kernel, cap), out_shape=(jax.ShapeDtypeS...]
where the time goes in v5:
time: 120 us
  Pallas kernels  116 us (97%)
  local copies, waits for them, and re-layouts  2.79 us (2%)
    pallas_call x1, Pallas kernels, run(): pl.pallas_call(functools.partial(kernel, cap), out_shape=(jax.ShapeDtypeS...  116 us
    unnamed x16, local copies, waits for them, and re-layouts  2.79 us

profile of v5, /device:TPU:1, one launch (start us, length us, event | category | flops | bytes accessed | tf_op | source)
XLA Modules:
  0.0 119.8 jit_solution(516599353253580669)
XLA Ops:
  0.0 0.0 copy-start.4
  0.0 0.0 copy-start
  0.0 0.7 copy-done.4
  0.7 0.7 copy.10.keep_ref
  1.4 0.0 copy-start.1
  1.4 0.0 copy-start.2
  1.4 116.3 %shard_map.75 = (f32[512,256]{1,0:T(8,128)S(1)}, s32[1,1]{1,0:T(1,128)}) custom-call(s32[8,4]{1,0:T(8,128)} %copy.10.keep_ref, f32[6]{0:T(128)} %amp_ref.1, f32[6]{0:T(128)} %width_ref.1, f32[3,4096]{1,0:T(4,128)} %centers_ref.1, f32[3,512]{1,0:T(4,128)} %sites_ref.1, f32[1,512]{1,0:T(1,128)} %bitcast.2, f32[512,256]{1,0:T(8,128)} %core_ref.1), custom_call_target="tpu_custom_call" | custom-call | tf_op jit(solution)/shard_map/pallas_call | solution.py:742
  118.3 0.0 copy-start.3
  118.3 0.0 copy-start.5
  118.3 0.0 copy-start.6
  118.3 0.0 copy-done
  118.3 0.0 copy-done.1
  118.3 0.0 copy-done.2
  118.4 0.6 copy-done.3
  119.0 0.0 copy-done.5
  119.0 0.0 copy-done.6
  119.0 0.8 copy.15
  (1 shorter events, 0.0 us)
Async XLA Ops:
  0.0 0.7 copy-start.4
  0.0 118.3 %copy-start = (f32[512,256]{1,0:T(8,128)S(1)}, f32[512,256]{1,0:T(8,128)}, u32[]{:S(2)}) copy-start(f32[512,256]{1,0:T(8,128)} %core_ref.1) | copy-start | bytes 1572868
  1.4 117.0 %copy-start.1 = (f32[3,4096]{1,0:T(4,128)S(1)}, f32[3,4096]{1,0:T(4,128)}, u32[]{:S(2)}) copy-start(f32[3,4096]{1,0:T(4,128)} %centers_ref.1) | copy-start | bytes 147460
  1.4 117.0 %copy-start.2 = (f32[3,512]{1,0:T(4,128)S(1)}, f32[3,512]{1,0:T(4,128)}, u32[]{:S(2)}) copy-start(f32[3,512]{1,0:T(4,128)} %sites_ref.1) | copy-start | bytes 18436
  118.3 0.7 copy-start.3
  118.3 0.7 copy-start.5
  118.3 0.7 copy-start.6
